TPU v7x, 32 devices: a whole 2x2x4 slice. The times are simulated.
32 devices in a mesh: gx: 4 (over x, core), gy: 2 (over y), gz: 4 (over z).
Axes of the slice: x: 2, y: 2, z: 4, core: 2. Of those that a mesh axis runs over, the one named last changes fastest.
Arguments:
- density: float32 [128, 512, 512], P('gz', 'gy', 'gx'), may hold values from 0.05 to 0.95
- design_mask: int32 [128, 512, 512], P('gz', 'gy', 'gx'), may hold values 0 or 1
- velocity: bfloat16 [3, 128, 512, 512], P(None, 'gz', 'gy', 'gx'), may hold values from -6 to 6
- adjoint_source: bfloat16 [3, 128, 512, 512], P(None, 'gz', 'gy', 'gx'), may hold values from -6 to 6
- adjoint_start: float32 [3, 128, 512, 512], P(None, 'gz', 'gy', 'gx'), may hold values from -4 to 4
Outputs:
- density_next: float32 [128, 512, 512], P('gz', 'gy', 'gx')
- adjoint: float32 [3, 128, 512, 512], P(None, 'gz', 'gy', 'gx')
All inputs are finite; a program needn't handle non-finite values. No bound on the sum of `design_mask` on one device may be relied on, other than what follows from the above.
Results may differ from a plain program's by a relative error of at most 0.0003.
Values sent between devices are 32-bit elements; how exact they have to be, the bound alone decides.
A program may use at most 256 MiB of HBM per device.

v0:
```python
import math

import jax
import jax.numpy as jnp
from jax import lax
from jax.sharding import PartitionSpec as P

NX = 512
NY = 512
RADIUS = 32
RADIUS_Z = 16
SWEEPS = 2


OMEGA = 0.8
ALPHA_MAX = 12.0
MOVE_STEP = 8.0
HIGH = lax.Precision.HIGHEST


def extended_2(cells, sides, width):
    for axis, dim in sides:
        count = lax.axis_size(axis)
        head = lax.slice_in_dim(cells, 0, width, axis=dim)
        tail = lax.slice_in_dim(cells, cells.shape[dim] - width, cells.shape[dim], axis=dim)
        cells = jnp.concatenate(
            [
                lax.ppermute(tail, axis, [(i, (i + 1) % count) for i in range(count)]),
                cells,
                lax.ppermute(head, axis, [((i + 1) % count, i) for i in range(count)]),
            ],
            axis=dim,
        )
    return cells


def jacobi_sweep(extended, source, diagonal):
    center = extended[:, 1:-1, 1:-1, 1:-1]
    beside = extended[:, 2:, 1:-1, 1:-1] + extended[:, :-2, 1:-1, 1:-1]
    beside = beside + extended[:, 1:-1, 2:, 1:-1] + extended[:, 1:-1, :-2, 1:-1]
    beside = beside + extended[:, 1:-1, 1:-1, 2:] + extended[:, 1:-1, 1:-1, :-2]
    return center + OMEGA * (source - (diagonal * center - beside)) / diagonal


def dft_tables(length):
    offsets = jnp.arange(length, dtype=jnp.int32)
    phases = (offsets[:, None] * offsets[None, :] % length).astype(jnp.float32) * (
        2.0 * math.pi / length
    )
    return (jnp.cos(phases), jnp.sin(phases))


def cone_spectrum(cos_x, cos_y):
    rows = jnp.arange(NY, dtype=jnp.int32)
    cols = jnp.arange(NX, dtype=jnp.int32)
    row_dist = jnp.minimum(rows, NY - rows).astype(jnp.float32)
    col_dist = jnp.minimum(cols, NX - cols).astype(jnp.float32)
    radial = jnp.sqrt(row_dist[:, None] ** 2 + col_dist[None, :] ** 2)
    weights = jnp.maximum(jnp.float32(RADIUS) - radial, jnp.float32(0.0))
    weights = weights / jnp.sum(weights)
    partial_x = jnp.dot(weights, cos_x, precision=HIGH, preferred_element_type=jnp.float32)
    spectrum = jnp.dot(cos_y, partial_x, precision=HIGH, preferred_element_type=jnp.float32)
    return spectrum / jnp.float32(NX * NY)


def faces_once(adjoint):
    return extended_2(adjoint, (("gx", 3), ("gy", 2), ("gz", 1)), 1)


def on_device(density, design_mask, velocity, adjoint_source, adjoint_start):
    resist = ALPHA_MAX * (1.0 - density) / (1.0 + density)
    diagonal = 6.0 + resist
    source = adjoint_source.astype(jnp.float32)
    adjoint = adjoint_start
    for sweep_index in range(SWEEPS):
        adjoint = jacobi_sweep(faces_once(adjoint), source, diagonal)
    slope = -2.0 * ALPHA_MAX / (1.0 + density) ** 2
    sensitivity = slope * jnp.sum(velocity.astype(jnp.float32) * adjoint, axis=0)
    depth, height, width = sensitivity.shape
    rimmed = extended_2(sensitivity, (("gz", 0),), RADIUS_Z)
    out_rows = jnp.arange(depth, dtype=jnp.int32)
    in_rows = jnp.arange(depth + 2 * RADIUS_Z, dtype=jnp.int32)
    offset = in_rows[None, :] - out_rows[:, None] - RADIUS_Z
    band = jnp.maximum(RADIUS_Z + 1 - jnp.abs(offset), 0).astype(jnp.float32) / jnp.float32(
        (RADIUS_Z + 1) ** 2
    )
    smoothed = jnp.einsum(
        "zw,wyx->zyx", band, rimmed, precision=HIGH, preferred_element_type=jnp.float32
    )
    blocks_x = lax.axis_size("gx")
    blocks_y = lax.axis_size("gy")
    groups = blocks_x * blocks_y
    planes = depth // groups
    sending = smoothed.reshape(groups, planes, 1, height, width)
    arrived = lax.all_to_all(sending, ("gx", "gy"), split_axis=0, concat_axis=2, tiled=True)
    gathered = arrived.reshape(planes, blocks_x, blocks_y, height, width)
    cos_x, sin_x = dft_tables(NX)
    cos_y, sin_y = dft_tables(NY)
    spectrum = cone_spectrum(cos_x, cos_y)
    cos_x3 = cos_x.reshape(blocks_x, width, NX)
    sin_x3 = sin_x.reshape(blocks_x, width, NX)
    cos_y3 = cos_y.reshape(blocks_y, height, NY)
    sin_y3 = sin_y.reshape(blocks_y, height, NY)

    def along_x(table):
        return jnp.einsum(
            "pabyx,axk->pbyk", gathered, table, precision=HIGH, preferred_element_type=jnp.float32
        )

    def along_y(field, table):
        return jnp.einsum(
            "pbyk,byq->pqk", field, table, precision=HIGH, preferred_element_type=jnp.float32
        )

    def back_y(field, table):
        return jnp.einsum(
            "pqk,byq->pbyk", field, table, precision=HIGH, preferred_element_type=jnp.float32
        )

    def back_x(field, table):
        return jnp.einsum(
            "pbyk,axk->pabyx", field, table, precision=HIGH, preferred_element_type=jnp.float32
        )

    x_real = along_x(cos_x3)
    x_imag = -along_x(sin_x3)
    y_real = along_y(x_real, cos_y3) + along_y(x_imag, sin_y3)
    y_imag = along_y(x_imag, cos_y3) - along_y(x_real, sin_y3)
    y_real = y_real * spectrum[None]
    y_imag = y_imag * spectrum[None]
    back_real = back_y(y_real, cos_y3) - back_y(y_imag, sin_y3)
    back_imag = back_y(y_imag, cos_y3) + back_y(y_real, sin_y3)
    result_planes = back_x(back_real, cos_x3) - back_x(back_imag, sin_x3)
    leaving = result_planes.reshape(1, planes, groups, height, width)
    returned = lax.all_to_all(leaving, ("gx", "gy"), split_axis=2, concat_axis=0, tiled=True)
    filtered = returned.reshape(depth, height, width)
    updated = jnp.clip(density - MOVE_STEP * filtered, 0.0, 1.0)
    density_next = jnp.where(design_mask == 1, jnp.zeros_like(updated), updated)
    return (density_next, adjoint)


def solution(mesh):
    return jax.shard_map(
        on_device,
        mesh=mesh,
        in_specs=(
            P("gz", "gy", "gx"),
            P("gz", "gy", "gx"),
            P(None, "gz", "gy", "gx"),
            P(None, "gz", "gy", "gx"),
            P(None, "gz", "gy", "gx"),
        ),
        out_specs=(P("gz", "gy", "gx"), P(None, "gz", "gy", "gx")),
        check_vma=False,
    )
```

profile of v0, /device:TPU:0, one launch (start us, length us, event | category | flops | bytes accessed | tf_op | source)
XLA Modules:
  0.0 804.3 jit_solution(6329805999736505006)
XLA Ops:
  0.6 21.2 %fusion.198 = (f32[3,32,256,1]{3,2,1,0:T(8,128)}, f32[3,32,256,1]{3,2,1,0:T(8,128)}) fusion(f32[3,32,256,128]{3,2,1,0:T(8,128)} %param.9), kind=kLoop, calls=%fused_computation.262 | loop fusion | bytes 393216 | tf_op jit(solution)/shard_map/slice | solution.py:24
  39.5 16.6 %copy.89 = f32[3,32,256,128]{3,1,2,0:T(8,128)} copy(f32[3,32,256,128]{3,2,1,0:T(8,128)} %param.9) | data formatting | bytes 25165824 | tf_op args[4]
  115.5 11.3 %collective-permute-done.5 = f32[3,1,258,130]{2,3,1,0:T(8,128)S(1)} collective-permute-done((f32[3,1,258,130]{2,3,1,0:T(8,128)S(1)}, f32[3,1,258,130]{2,3,1,0:T(8,128)S(1)}, u32[]{:S(2)}, u32[]{:S(2)}) %collective-permute-start.5) | collective-permute-done | bytes 402512 | tf_op jit(solution)/shard_map/ppermute | solution.py:28
  127.5 88.7 %fusion.2 = f32[3,32,256,128]{3,1,2,0:T(8,128)} fusion(f32[3,32,256,128]{3,1,2,0:T(8,128)} %copy.89, f32[3,32,256,1]{3,1,2,0:T(8,128)} %copy.78, f32[3,32,256,1]{3,1,2,0:T(8,128)} %copy.80, f32[3,32,1,130]{3,1,2,0:T(8,128)} %copy-done.5, f32[3,32,1,130]{3,1,2,0:T(8,128)} %copy-done.7, f32[3,1,258,130]{3,1,2,0:T(1,128)S(1)} %copy.84, ...), kind=kLoop, calls=%fused_computation.4 | loop fusion | flops 94371840 | bytes 36752992 | tf_op jit(solution)/shard_map/add | solution.py:42
  216.2 21.1 %fusion.197 = (f32[3,32,256,1]{3,1,2,0:T(8,128)}, f32[3,32,256,1]{3,1,2,0:T(8,128)}) fusion(f32[3,32,256,128]{3,1,2,0:T(8,128)} %fusion.2), kind=kLoop, calls=%fused_computation.261 | loop fusion | bytes 393216 | tf_op jit(solution)/shard_map/slice | solution.py:24
  298.4 14.0 %collective-permute-done.10 = f32[3,1,258,130]{2,3,1,0:T(8,128)S(1)} collective-permute-done((f32[3,1,258,130]{2,3,1,0:T(8,128)S(1)}, f32[3,1,258,130]{2,3,1,0:T(8,128)S(1)}, u32[]{:S(2)}, u32[]{:S(2)}) %collective-permute-start.10) | collective-permute-done | bytes 402512 | tf_op jit(solution)/shard_map/ppermute | solution.py:30
  323.9 94.7 %multiply_reduce_fusion = (f32[32,256,128]{2,0,1:T(8,128)}, f32[3,32,256,128]{3,1,2,0:T(8,128)}) fusion(bf16[3,32,256,128]{3,2,1,0:T(8,128)(2,1)} %param.7, f32[3,32,256,128]{3,1,2,0:T(8,128)} %fusion.2, f32[3,32,256,1]{3,1,2,0:T(8,128)} %copy.92, f32[3,32,256,1]{3,1,2,0:T(8,128)} %copy.93, f32[3,32,1,130]{3,1,2,0:T(8,128)} %copy-done.4, ...), kind=kLoop, calls=%fused_computation.56 | loop fusion | flops 102760448 | bytes 47238752 | tf_op jit(solution)/shard_map/reduce_sum | solution.py:78
  429.1 46.4 %collective-permute-done.12 = f32[16,256,128]{2,0,1:T(8,128)S(1)} collective-permute-done((f32[16,256,128]{2,0,1:T(8,128)S(1)}, f32[16,256,128]{2,0,1:T(8,128)S(1)}, u32[]{:S(2)}, u32[]{:S(2)}) %collective-permute-start.12) | collective-permute-done | bytes 2097184 | tf_op jit(solution)/shard_map/ppermute | solution.py:28
  475.5 41.5 %collective-permute-done.13 = f32[16,256,128]{2,0,1:T(8,128)S(1)} collective-permute-done((f32[16,256,128]{2,0,1:T(8,128)S(1)}, f32[16,256,128]{2,0,1:T(8,128)S(1)}, u32[]{:S(2)}, u32[]{:S(2)}) %collective-permute-start.13) | collective-permute-done | bytes 2097184 | tf_op jit(solution)/shard_map/ppermute | solution.py:30
  547.7 34.4 %all-to-all-done = f32[8,4,1,256,128]{4,3,1,2,0:T(8,128)} async-done(((f32[8,4,1,256,128]{4,3,1,2,0:T(8,128)}), f32[8,4,1,256,128]{4,3,1,2,0:T(8,128)}, u32[]{:S(2)}, u32[]{:S(2)}) %all-to-all-start) | async-done | bytes 4194336 | tf_op jit(solution)/shard_map/all_to_all | solution.py:95
  582.1 13.3 %fusion.48 = f32[4,2,256,512,1]{3,2,4,1,0:T(8,128)S(1)} fusion(f32[4,4,2,256,128]{4,3,0,2,1:T(8,128)} %bitcast.9, s32[4,128]{1,0:T(4,128)S(1)} %multiply_add_fusion.1), kind=kOutput, calls=%fused_computation.96 | convolution fusion | flops 6446120960 | bytes 8390656 | tf_op jit(solution)/shard_map/pabyx,axk->pbyk/dot_general | solution.py:106
  595.4 13.7 %fusion.46 = f32[4,2,256,512,1]{3,2,4,1,0:T(8,128)S(1)} fusion(f32[4,4,2,256,128]{4,3,0,2,1:T(8,128)} %bitcast.9, s32[4,128]{1,0:T(4,128)S(1)} %multiply_add_fusion.1), kind=kOutput, calls=%fused_computation.94 | convolution fusion | flops 6446120960 | bytes 8390656 | tf_op jit(solution)/shard_map/pabyx,axk->pbyk/dot_general | solution.py:106
  609.2 11.7 %fusion.40 = f32[512,4,512,1]{2,0,3,1:T(8,128)S(1)} fusion(f32[4,2,256,512,1]{3,2,4,1,0:T(8,128)S(1)} %fusion.48, s32[2,256]{1,0:T(2,128)S(1)} %multiply_add_fusion), kind=kOutput, calls=%fused_computation.82 | convolution fusion | flops 6446120960 | bytes 8390656 | tf_op jit(solution)/shard_map/pbyk,byq->pqk/dot_general | solution.py:111
  620.9 11.5 %fusion.38 = f32[512,4,512,1]{2,0,3,1:T(8,128)S(1)} fusion(f32[4,2,256,512,1]{3,2,4,1,0:T(8,128)S(1)} %fusion.48, s32[2,256]{1,0:T(2,128)S(1)} %multiply_add_fusion), kind=kOutput, calls=%fused_computation.80 | convolution fusion | flops 6446120960 | bytes 8390656 | tf_op jit(solution)/shard_map/pbyk,byq->pqk/dot_general | solution.py:111
  632.5 12.1 %fusion.37 = f32[512,4,512]{2,0,1:T(8,128)S(1)} fusion(f32[512,4,512,1]{2,0,3,1:T(8,128)S(1)} %fusion.40, f32[4,2,256,512,1]{3,2,4,1,0:T(8,128)S(1)} %fusion.46, f32[512,512]{1,0:T(8,128)S(1)} %convolution_multiply_fusion, s32[2,256]{1,0:T(2,128)S(1)} %multiply_add_fusion), kind=kOutput, calls=%fused_computation.78 | convolution fusion | flops 6449266688 | bytes 13633536 | tf_op jit(solution)/shard_map/pbyk,byq->pqk/dot_general | solution.py:111
  644.6 11.4 %fusion.28 = f32[2,256,4,512]{3,1,0,2:T(8,128)S(1)} fusion(f32[512,4,512]{2,0,1:T(8,128)S(1)} %fusion.37, s32[2,256]{1,0:T(2,128)S(1)} %multiply_add_fusion), kind=kOutput, calls=%fused_computation.67 | convolution fusion | flops 6446120960 | bytes 8390656 | tf_op jit(solution)/shard_map/pqk,byq->pbyk/dot_general | solution.py:116
  656.0 11.1 %fusion.30 = f32[2,256,4,512]{3,1,0,2:T(8,128)S(1)} fusion(f32[512,4,512]{2,0,1:T(8,128)S(1)} %fusion.37, s32[2,256]{1,0:T(2,128)S(1)} %multiply_add_fusion), kind=kOutput, calls=%fused_computation.69 | convolution fusion | flops 6446120960 | bytes 8390656 | tf_op jit(solution)/shard_map/pqk,byq->pbyk/dot_general | solution.py:116
  667.2 12.2 %fusion.36 = f32[512,4,512]{2,0,1:T(8,128)S(1)} fusion(f32[512,4,512,1]{2,0,3,1:T(8,128)S(1)} %fusion.38, f32[4,2,256,512,1]{3,2,4,1,0:T(8,128)S(1)} %fusion.46, f32[512,512]{1,0:T(8,128)S(1)} %convolution_multiply_fusion, s32[2,256]{1,0:T(2,128)S(1)} %multiply_add_fusion), kind=kOutput, calls=%fused_computation.76 | convolution fusion | flops 6449266688 | bytes 13633536 | tf_op jit(solution)/shard_map/pbyk,byq->pqk/dot_general | solution.py:111
  679.4 11.0 %fusion.32 = f32[2,256,4,512]{3,1,0,2:T(8,128)S(1)} fusion(f32[512,4,512]{2,0,1:T(8,128)S(1)} %fusion.36, s32[2,256]{1,0:T(2,128)S(1)} %multiply_add_fusion), kind=kOutput, calls=%fused_computation.71 | convolution fusion | flops 6446120960 | bytes 8390656 | tf_op jit(solution)/shard_map/pqk,byq->pbyk/dot_general | solution.py:116
  690.4 11.4 %fusion.34 = f32[2,256,4,512]{3,1,0,2:T(8,128)S(1)} fusion(f32[512,4,512]{2,0,1:T(8,128)S(1)} %fusion.36, s32[2,256]{1,0:T(2,128)S(1)} %multiply_add_fusion), kind=kOutput, calls=%fused_computation.73 | convolution fusion | flops 6446120960 | bytes 8390656 | tf_op jit(solution)/shard_map/pqk,byq->pbyk/dot_general | solution.py:116
  701.7 11.3 %fusion.24 = f32[4,128,4,2,256]{4,1,3,2,0:T(8,128)S(1)} fusion(f32[2,256,4,512]{3,1,0,2:T(8,128)S(1)} %fusion.32, f32[2,256,4,512]{3,1,0,2:T(8,128)S(1)} %fusion.28, s32[4,128]{1,0:T(4,128)S(1)} %multiply_add_fusion.1), kind=kOutput, calls=%fused_computation.63 | convolution fusion | flops 6447169536 | bytes 12584960 | tf_op jit(solution)/shard_map/pbyk,axk->pabyx/dot_general | solution.py:121
  713.1 13.2 %subtract_bitcast_fusion = f32[4,4,2,256,128]{3,4,2,0,1:T(8,128)} fusion(f32[4,128,4,2,256]{4,1,3,2,0:T(8,128)S(1)} %fusion.24, f32[2,256,4,512]{3,1,0,2:T(8,128)S(1)} %fusion.30, f32[2,256,4,512]{3,1,0,2:T(8,128)S(1)} %fusion.34, s32[4,128]{1,0:T(4,128)S(1)} %multiply_add_fusion.1), kind=kOutput, calls=%fused_computation.87 | convolution fusion | flops 6448218112 | bytes 16779264 | tf_op jit(solution)/shard_map/pbyk,axk->pabyx/dot_general | solution.py:121
  741.1 16.6 %copy.115 = f32[3,32,256,128]{3,2,1,0:T(8,128)} copy(f32[3,32,256,128]{3,1,2,0:T(8,128)} %get-tuple-element.11) | data formatting | bytes 25165824
  757.7 31.2 %all-to-all-done.1 = f32[1,4,8,256,128]{4,3,1,0,2:T(8,128)} async-done(((f32[1,4,8,256,128]{4,3,1,0,2:T(8,128)}), f32[1,4,8,256,128]{4,3,1,0,2:T(8,128)}, u32[]{:S(2)}, u32[]{:S(2)}) %all-to-all-start.1) | async-done | bytes 4194336 | tf_op jit(solution)/shard_map/all_to_all | solution.py:135
  (79 shorter events, 221.5 us)
Async XLA Ops:
  29.4 26.7 %collective-permute-start = (f32[3,32,256,1]{2,1,3,0:T(8,128)S(1)}, f32[3,32,256,1]{2,1,3,0:T(8,128)S(1)}, u32[]{:S(2)}, u32[]{:S(2)}) collective-permute-start(f32[3,32,256,1]{2,1,3,0:T(8,128)S(1)} %copy.139), channel_id=1, source_target_pairs={{0,8},{8,16},{16,24},{24,0},{1,9},{9,17},{17,25},{25,1},{2,10},{10... | collective-permute-start | bytes 294920 | tf_op jit(solution)/shard_map/ppermute | solution.py:28
  37.5 29.6 %collective-permute-start.1 = (f32[3,32,256,1]{2,1,3,0:T(8,128)S(1)}, f32[3,32,256,1]{2,1,3,0:T(8,128)S(1)}, u32[]{:S(2)}, u32[]{:S(2)}) collective-permute-start(f32[3,32,256,1]{2,1,3,0:T(8,128)S(1)} %copy.140), channel_id=1, source_target_pairs={{8,0},{16,8},{24,16},{0,24},{9,1},{17,9},{25,17},{1,25},{10,2},{18... | collective-permute-start | bytes 294920 | tf_op jit(solution)/shard_map/ppermute | solution.py:30
  77.6 8.8 %copy-start = (f32[3,32,256,1]{3,1,2,0:T(8,128)S(1)}, f32[3,32,256,1]{3,1,2,0:T(8,128)}, u32[]{:S(2)}) copy-start(f32[3,32,256,1]{3,1,2,0:T(8,128)} %copy.80) | copy-start | bytes 294916
  78.8 6.0 collective-permute-start.2
  81.2 5.2 collective-permute-start.3
  84.8 10.7 %copy-start.5 = (f32[3,32,1,130]{3,1,2,0:T(8,128)}, f32[3,32,1,130]{3,1,2,0:T(8,128)S(1)}, u32[]{:S(2)}) copy-start(f32[3,32,1,130]{3,1,2,0:T(8,128)S(1)} %collective-permute-done.2) | copy-start | bytes 149764
  86.4 9.2 %copy-start.7 = (f32[3,32,1,130]{3,1,2,0:T(8,128)}, f32[3,32,1,130]{3,1,2,0:T(8,128)S(1)}, u32[]{:S(2)}) copy-start(f32[3,32,1,130]{3,1,2,0:T(8,128)S(1)} %collective-permute-done.3) | copy-start | bytes 149764
  96.1 18.3 %collective-permute-start.4 = (f32[3,1,258,130]{2,3,1,0:T(8,128)S(1)}, f32[3,1,258,130]{2,3,1,0:T(8,128)S(1)}, u32[]{:S(2)}, u32[]{:S(2)}) collective-permute-start(f32[3,1,258,130]{2,3,1,0:T(8,128)S(1)} %copy.81), channel_id=1, source_target_pairs={{1,0},{2,1},{3,2},{0,3},{5,4},{6,5},{7,6},{4,7},{9,8},{10,9},{11,1... | collective-permute-start | bytes 1207448 | tf_op jit(solution)/shard_map/ppermute | solution.py:30
  100.3 26.6 %collective-permute-start.5 = (f32[3,1,258,130]{2,3,1,0:T(8,128)S(1)}, f32[3,1,258,130]{2,3,1,0:T(8,128)S(1)}, u32[]{:S(2)}, u32[]{:S(2)}) collective-permute-start(f32[3,1,258,130]{2,3,1,0:T(8,128)S(1)} %copy.83), channel_id=1, source_target_pairs={{0,1},{1,2},{2,3},{3,0},{4,5},{5,6},{6,7},{7,4},{8,9},{9,10},{10,1... | collective-permute-start | bytes 1207448 | tf_op jit(solution)/shard_map/ppermute | solution.py:28
  246.4 10.9 %collective-permute-start.6 = (f32[3,32,256,1]{2,1,3,0:T(8,128)S(1)}, f32[3,32,256,1]{2,1,3,0:T(8,128)S(1)}, u32[]{:S(2)}, u32[]{:S(2)}) collective-permute-start(f32[3,32,256,1]{2,1,3,0:T(8,128)S(1)} %copy.90), channel_id=1, source_target_pairs={{0,8},{8,16},{16,24},{24,0},{1,9},{9,17},{17,25},{25,1},{2,10},{10... | collective-permute-start | bytes 294920 | tf_op jit(solution)/shard_map/ppermute | solution.py:28
  255.5 12.5 %collective-permute-start.7 = (f32[3,32,256,1]{2,1,3,0:T(8,128)S(1)}, f32[3,32,256,1]{2,1,3,0:T(8,128)S(1)}, u32[]{:S(2)}, u32[]{:S(2)}) collective-permute-start(f32[3,32,256,1]{2,1,3,0:T(8,128)S(1)} %copy.91), channel_id=1, source_target_pairs={{8,0},{16,8},{24,16},{0,24},{9,1},{17,9},{25,17},{1,25},{10,2},{18... | collective-permute-start | bytes 294920 | tf_op jit(solution)/shard_map/ppermute | solution.py:30
  278.5 7.2 copy-start.1
  279.8 4.7 collective-permute-start.8
  281.1 4.6 collective-permute-start.9
  284.4 10.4 %copy-start.4 = (f32[3,32,1,130]{3,1,2,0:T(8,128)}, f32[3,32,1,130]{3,1,2,0:T(8,128)S(1)}, u32[]{:S(2)}) copy-start(f32[3,32,1,130]{3,1,2,0:T(8,128)S(1)} %collective-permute-done.8) | copy-start | bytes 149764
  285.7 9.2 %copy-start.6 = (f32[3,32,1,130]{3,1,2,0:T(8,128)}, f32[3,32,1,130]{3,1,2,0:T(8,128)S(1)}, u32[]{:S(2)}) copy-start(f32[3,32,1,130]{3,1,2,0:T(8,128)S(1)} %collective-permute-done.9) | copy-start | bytes 149764
  295.4 16.9 %collective-permute-start.10 = (f32[3,1,258,130]{2,3,1,0:T(8,128)S(1)}, f32[3,1,258,130]{2,3,1,0:T(8,128)S(1)}, u32[]{:S(2)}, u32[]{:S(2)}) collective-permute-start(f32[3,1,258,130]{2,3,1,0:T(8,128)S(1)} %copy.94), channel_id=1, source_target_pairs={{1,0},{2,1},{3,2},{0,3},{5,4},{6,5},{7,6},{4,7},{9,8},{10,9},{11,1... | collective-permute-start | bytes 1207448 | tf_op jit(solution)/shard_map/ppermute | solution.py:30
  298.3 24.9 %collective-permute-start.11 = (f32[3,1,258,130]{2,3,1,0:T(8,128)S(1)}, f32[3,1,258,130]{2,3,1,0:T(8,128)S(1)}, u32[]{:S(2)}, u32[]{:S(2)}) collective-permute-start(f32[3,1,258,130]{2,3,1,0:T(8,128)S(1)} %copy.96), channel_id=1, source_target_pairs={{0,1},{1,2},{2,3},{3,0},{4,5},{5,6},{6,7},{7,4},{8,9},{9,10},{10,1... | collective-permute-start | bytes 1207448 | tf_op jit(solution)/shard_map/ppermute | solution.py:28
  425.0 50.5 %collective-permute-start.12 = (f32[16,256,128]{2,0,1:T(8,128)S(1)}, f32[16,256,128]{2,0,1:T(8,128)S(1)}, u32[]{:S(2)}, u32[]{:S(2)}) collective-permute-start(f32[16,256,128]{2,0,1:T(8,128)S(1)} %get-tuple-element.24), channel_id=1, source_target_pairs={{0,1},{1,2},{2,3},{3,0},{4,5},{5,6},{6,7},{7,4},{8,9},{9,10},{10,1... | collective-permute-start | bytes 6291464 | tf_op jit(solution)/shard_map/ppermute | solution.py:28
  426.8 90.2 %collective-permute-start.13 = (f32[16,256,128]{2,0,1:T(8,128)S(1)}, f32[16,256,128]{2,0,1:T(8,128)S(1)}, u32[]{:S(2)}, u32[]{:S(2)}) collective-permute-start(f32[16,256,128]{2,0,1:T(8,128)S(1)} %get-tuple-element.25), channel_id=1, source_target_pairs={{1,0},{2,1},{3,2},{0,3},{5,4},{6,5},{7,6},{4,7},{9,8},{10,9},{11,1... | collective-permute-start | bytes 6291464 | tf_op jit(solution)/shard_map/ppermute | solution.py:30
  526.4 55.7 %all-to-all-start = ((f32[8,4,1,256,128]{4,3,1,2,0:T(8,128)}), f32[8,4,1,256,128]{4,3,1,2,0:T(8,128)}, u32[]{:S(2)}, u32[]{:S(2)}) async-start(f32[8,4,1,256,128]{4,3,1,2,0:T(8,128)} %copy.102), calls=%async_computation | async-start | bytes 8388608 | tf_op jit(solution)/shard_map/all_to_all | solution.py:95
  736.1 52.8 %all-to-all-start.1 = ((f32[1,4,8,256,128]{4,3,1,0,2:T(8,128)}), f32[1,4,8,256,128]{4,3,1,0,2:T(8,128)}, u32[]{:S(2)}, u32[]{:S(2)}) async-start(f32[1,4,8,256,128]{4,3,1,0,2:T(8,128)} %copy.111), calls=%async_computation.1 | async-start | bytes 8388608 | tf_op jit(solution)/shard_map/all_to_all | solution.py:135
  788.9 5.4 copy-start.2
  788.9 5.4 copy-start.3
where the time goes:
time: 812 us; the launch traced here: 804 us
  other arithmetic  226 us (28%)
  waiting for transfers between devices  205 us (25%)
  local copies, waits for them, and re-layouts  179 us (22%)
  matrix products  162 us (20%)
  starting transfers between devices  31.7 us (4%)
    reduce_sum x1, other arithmetic, on_device(): jnp.sum(velocity.astype(jnp.float32) * adjoint, axis=0)  94.7 us
    add x1, other arithmetic, jacobi_sweep(): return center + OMEGA * (source - (diagonal * center - beside)) / diagonal  88.7 us
    ppermute x7, waiting for transfers between devices, extended_2(): lax.ppermute(tail, axis, [(i, (i + 1) % count) for i in range(count)])  73.7 us
    ppermute x7, waiting for transfers between devices, extended_2(): lax.ppermute(head, axis, [((i + 1) % count, i) for i in range(count)])  65.3 us
    unnamed x21, local copies, waits for them, and re-layouts  52.9 us
    slice x5, local copies, waits for them, and re-layouts, extended_2(): head = lax.slice_in_dim(cells, 0, width, axis=dim)  52.4 us
    dot_general x4, matrix products, along_y(): jnp.einsum('pbyk,byq->pqk', field, table, precision=HIGH, preferred_eleme...  47.6 us
    dot_general x4, matrix products, back_y(): jnp.einsum('pqk,byq->pbyk', field, table, precision=HIGH, preferred_eleme...  44.9 us
  transfers between devices with their start and end apart: 16, of which 12 were waited for; matrix products, arithmetic and copies ran while one was open for 12% of the time, Pallas kernels for 0%

commit v1 on v0

v1 whole, which is shorter than its diff:
```python
import functools
import math

import jax
import jax.numpy as jnp
import ml_dtypes
import numpy as np
from jax import lax
from jax.experimental import pallas as pl
from jax.experimental.pallas import tpu as pltpu
from jax.sharding import PartitionSpec as P

NX = 512
NY = 512
RADIUS = 32
RADIUS_Z = 16
OMEGA = 0.8
ALPHA_MAX = 12.0
MOVE_STEP = 8.0
GROUP = 4
LANES = 128
VMEM = 48 * 2**20


def params():
    return pltpu.CompilerParams(
        vmem_limit_bytes=VMEM, dimension_semantics=("arbitrary",)
    )


def cost(flops, size):
    return pl.CostEstimate(flops=int(flops), bytes_accessed=int(size), transcendentals=0)


def to_next(array, axis):
    count = lax.axis_size(axis)
    return lax.ppermute(array, axis, [(i, (i + 1) % count) for i in range(count)])


def to_prev(array, axis):
    count = lax.axis_size(axis)
    return lax.ppermute(array, axis, [((i + 1) % count, i) for i in range(count)])


def pack_faces(plane, lane, column, xlo, xhi, ylo, yhi):
    height = plane.shape[0]
    here = lane == column
    xlo[...] = jnp.where(here, pltpu.roll(plane, column, 1), xlo[...])
    xhi[...] = jnp.where(here, pltpu.roll(plane, column + 1, 1), xhi[...])
    ylo[pl.ds(column, 1), :] = plane[0:1]
    yhi[pl.ds(column, 1), :] = plane[height - 1 : height]


def faces_kernel(depth, adj, xlo, xhi, ylo, yhi):
    step = pl.program_id(0)

    @pl.when(step == 0)
    def _():
        for ref in (xlo, xhi, ylo, yhi):
            ref[...] = jnp.zeros_like(ref)

    lane = lax.broadcasted_iota(jnp.int32, xlo.shape, 1)
    for j in range(GROUP):
        for c in range(3):
            pack_faces(
                adj[c, j], lane, c * depth + step * GROUP + j, xlo, xhi, ylo, yhi
            )


def face_shapes(depth, height):
    return [jax.ShapeDtypeStruct((height, LANES), jnp.float32)] * 2 + [
        jax.ShapeDtypeStruct((3 * depth, LANES), jnp.float32)
    ] * 2


def whole_spec(shape):
    return pl.BlockSpec(shape, lambda i: (0,) * len(shape))


def faces_of(adjoint):
    _, depth, height, width = adjoint.shape
    shapes = face_shapes(depth, height)
    return pl.pallas_call(
        functools.partial(faces_kernel, depth),
        grid=(depth // GROUP,),
        in_specs=[pl.BlockSpec((3, GROUP, height, width), lambda i: (0, i, 0, 0))],
        out_specs=[whole_spec(s.shape) for s in shapes],
        out_shape=shapes,
        compiler_params=params(),
        cost_estimate=cost(10 * adjoint.size, 4 * adjoint.size),
        name="faces",
    )(adjoint)


def sweep_kernel(conf, *refs):
    depth, first, stride, use_lo, use_hi, faces, fresh, sens = conf
    refs = list(refs)
    adj, prev, follow, source, density, xleft, xright, yabove, ybelow = refs[:9]
    refs = refs[9:]
    zlo = refs.pop(0) if use_lo else None
    zhi = refs.pop(0) if use_hi else None
    velocity = refs.pop(0) if sens else None
    if faces and not fresh:
        held = refs[:4]
        refs = refs[4:]
    aliased = conf.aliased
    refs = refs[aliased:]
    out = refs.pop(0)
    if faces:
        packs = refs[:4]
        refs = refs[4:]
    if sens:
        sens_out, pack_lo, pack_hi = refs
    step = pl.program_id(0)
    block = first + stride * step
    height, width = out.shape[2:]
    if faces:

        @pl.when(step == 0)
        def _():
            for at in range(4):
                if fresh:
                    packs[at][...] = jnp.zeros_like(packs[at])
                else:
                    packs[at][...] = held[at][...]

    lane = lax.broadcasted_iota(jnp.int32, (height, width), 1)
    row = lax.broadcasted_iota(jnp.int32, (height, width), 0)
    last_block = depth // GROUP - 1
    for j in range(GROUP):
        dens = density[j]
        weight = OMEGA * (1.0 + dens) / (18.0 - 6.0 * dens)
        total = None
        for c in range(3):
            column = c * depth + block * GROUP + j
            plane = adj[c, j]
            if j > 0:
                below = adj[c, j - 1]
            else:
                below = prev[c, 0]
                if use_lo:
                    below = jnp.where(block == 0, zlo[c], below)
            if j < GROUP - 1:
                above = adj[c, j + 1]
            else:
                above = follow[c, 0]
                if use_hi:
                    above = jnp.where(block == last_block, zhi[c], above)
            beside = above + below
            beside += jnp.where(
                row == 0, yabove[pl.ds(column, 1), :], pltpu.roll(plane, 1, 0)
            )
            beside += jnp.where(
                row == height - 1,
                ybelow[pl.ds(column, 1), :],
                pltpu.roll(plane, height - 1, 0),
            )
            beside += jnp.where(
                lane == 0,
                pltpu.roll(xleft[...], (LANES - column) % LANES, 1),
                pltpu.roll(plane, 1, 1),
            )
            beside += jnp.where(
                lane == width - 1,
                pltpu.roll(xright[...], LANES - 1 - column, 1),
                pltpu.roll(plane, width - 1, 1),
            )
            relaxed = (1.0 - OMEGA) * plane + weight * (
                source[c, j].astype(jnp.float32) + beside
            )
            out[c, j] = relaxed
            if faces:
                pack_faces(relaxed, lane, column, *packs)
            if sens:
                part = velocity[c, j].astype(jnp.float32) * relaxed
                total = part if total is None else total + part
        if sens:
            near = 1.0 / (1.0 + dens)
            value = (-2.0 * ALPHA_MAX) * near * near * total
            sens_out[j] = value
            turned = pltpu.roll(value, RADIUS * (j + 1) % LANES, 1)
            group = lane // RADIUS
            low = jnp.where(group == (j + 1) % GROUP, turned, 0.0)
            high = jnp.where(group == j, turned, 0.0)
            if j == 0:
                pack_lo[0] = low
                pack_hi[0] = high
            else:
                pack_lo[0] += low
                pack_hi[0] += high


class Conf(tuple):
    aliased = 0


def sweep(
    adjoint,
    source,
    density,
    arrived,
    first,
    count,
    stride=1,
    zlo=None,
    zhi=None,
    faces=False,
    held=None,
    velocity=None,
    sens_base=0,
    onto=(),
):
    _, depth, height, width = adjoint.shape
    sens = velocity is not None
    conf = Conf(
        (depth, first, stride, zlo is not None, zhi is not None, faces, held is None, sens)
    )
    conf.aliased = len(onto)

    def at(i):
        return first + stride * i

    block = pl.BlockSpec((3, GROUP, height, width), lambda i: (0, at(i), 0, 0))
    plane_shape = (3, 1, height, width)
    operands = [adjoint, adjoint, adjoint, source, density, *arrived]
    in_specs = [
        block,
        pl.BlockSpec(plane_shape, lambda i: (0, jnp.maximum(at(i) * GROUP - 1, 0), 0, 0)),
        pl.BlockSpec(
            plane_shape, lambda i: (0, jnp.minimum(at(i) * GROUP + GROUP, depth - 1), 0, 0)
        ),
        block,
        pl.BlockSpec((GROUP, height, width), lambda i: (at(i), 0, 0)),
    ]
    in_specs += [whole_spec(a.shape) for a in arrived]
    for face in (zlo, zhi):
        if face is not None:
            operands.append(face)
            in_specs.append(whole_spec(face.shape))
    if sens:
        operands.append(velocity)
        in_specs.append(block)
    if held is not None:
        operands += list(held)
        in_specs += [whole_spec(a.shape) for a in held]
    aliases = {}
    for index, array in onto:
        aliases[len(operands)] = index
        operands.append(array)
        in_specs.append(pl.BlockSpec(memory_space=pl.ANY))
    out_specs = [block]
    out_shape = [jax.ShapeDtypeStruct(adjoint.shape, jnp.float32)]
    if faces:
        shapes = face_shapes(depth, height)
        out_shape += shapes
        out_specs += [whole_spec(s.shape) for s in shapes]
    if sens:
        half = depth // 2
        out_shape += [jax.ShapeDtypeStruct((half, height, width), jnp.float32)] + [
            jax.ShapeDtypeStruct((half // GROUP, height, LANES), jnp.float32)
        ] * 2
        out_specs += [
            pl.BlockSpec((GROUP, height, width), lambda i: (at(i) - sens_base, 0, 0))
        ] + [pl.BlockSpec((1, height, LANES), lambda i: (at(i) - sens_base, 0, 0))] * 2
    cells = 3 * GROUP * count * height * width
    return pl.pallas_call(
        functools.partial(sweep_kernel, conf),
        grid=(count,),
        in_specs=in_specs,
        out_specs=out_specs,
        out_shape=out_shape,
        input_output_aliases=aliases,
        compiler_params=params(),
        cost_estimate=cost(40 * cells, 14 * cells),
        name="sweep",
    )(*operands)


def parts_of(table):
    high = table.astype(ml_dtypes.bfloat16)
    low = (table - high.astype(np.float64)).astype(ml_dtypes.bfloat16)
    return jnp.asarray(high), jnp.asarray(low)


def real_dft(length):
    half = length // 2
    waves = np.concatenate([np.arange(half + 1), np.arange(1, half)])
    phase = 2.0 * math.pi / length * (waves[:, None] * np.arange(length)[None, :] % length)
    table = np.where(np.arange(length)[:, None] <= half, np.cos(phase), np.sin(phase))
    scale = np.full((length, 1), math.sqrt(2.0 / length))
    scale[0] = scale[half] = math.sqrt(1.0 / length)
    return table * scale, waves


def cone_tables(height, width):
    long_x = -(-(width + 2 * RADIUS) // LANES) * LANES
    long_y = height + 2 * RADIUS
    basis_x, waves_x = real_dft(long_x)
    basis_y, waves_y = real_dft(long_y)
    reach = np.arange(-RADIUS, RADIUS + 1)
    cone = np.maximum(0.0, RADIUS - np.sqrt(reach[:, None] ** 2.0 + reach[None, :] ** 2.0))
    cone = cone / np.sum(cone)
    cos_y = np.cos(2.0 * math.pi / long_y * waves_y[:, None] * reach[None, :])
    cos_x = np.cos(2.0 * math.pi / long_x * waves_x[:, None] * reach[None, :])
    spectrum = (cos_y @ cone @ cos_x.T).astype(np.float32)
    into_x = np.zeros((GROUP, width + LANES, long_x))
    for j in range(GROUP):
        into_x[j, :width] = basis_x[:, RADIUS : RADIUS + width].T
        left = width + RADIUS * j
        into_x[j, left : left + RADIUS] = basis_x[:, :RADIUS].T
        right = width + RADIUS * ((j + 1) % GROUP)
        into_x[j, right : right + RADIUS] = basis_x[:, RADIUS + width : 2 * RADIUS + width].T
    tables = [
        *parts_of(into_x),
        *parts_of(basis_y),
        *parts_of(basis_y[:, RADIUS : RADIUS + height].T),
        *parts_of(basis_x[:, RADIUS : RADIUS + width]),
        jnp.asarray(spectrum),
    ]
    return tables


def split(value):
    high = value.astype(jnp.bfloat16)
    return high, (value - high.astype(jnp.float32)).astype(jnp.bfloat16)


def product(left, right):
    dot = functools.partial(jnp.dot, preferred_element_type=jnp.float32)
    return dot(left[0], right[0]) + (dot(left[0], right[1]) + dot(left[1], right[0]))


def cone_kernel(
    own, left, right,
    above, above_left, above_right,
    below, below_left, below_right,
    into_high, into_low, y_high, y_low, yback_high, yback_low, xback_high, xback_low,
    spectrum, out,
):
    for j in range(GROUP):

        def wide(mid, lhs, rhs):
            group = lax.broadcasted_iota(jnp.int32, lhs.shape, 1) // RADIUS
            return jnp.concatenate([mid, jnp.where(group == j, lhs, rhs)], axis=1)

        cells = jnp.concatenate(
            [
                wide(above[j], above_left[0], above_right[0]),
                wide(own[j], left[0], right[0]),
                wide(below[j], below_left[0], below_right[0]),
            ],
            axis=0,
        )
        waves = product(split(cells), (into_high[j], into_low[j]))
        waves = product((y_high[...], y_low[...]), split(waves)) * spectrum[...]
        rows = product((yback_high[...], yback_low[...]), split(waves))
        out[j] = product(split(rows), (xback_high[...], xback_low[...]))


def cone_filter(sens, pack_lo, pack_hi, tables):
    planes, height, width = sens.shape
    steps = planes // GROUP
    left = to_next(pack_hi, "gx")
    right = to_prev(pack_lo, "gx")
    strips = [sens, left, right]
    above = to_next(
        jnp.concatenate([s[:, height - RADIUS :] for s in strips], axis=0), "gy"
    )
    below = to_prev(jnp.concatenate([s[:, :RADIUS] for s in strips], axis=0), "gy")
    packed = pl.BlockSpec((1, height, LANES), lambda i: (i, 0, 0))
    strip_specs = [
        pl.BlockSpec((GROUP, RADIUS, width), lambda i: (i, 0, 0)),
        pl.BlockSpec((1, RADIUS, LANES), lambda i: (planes + i, 0, 0)),
        pl.BlockSpec((1, RADIUS, LANES), lambda i: (planes + steps + i, 0, 0)),
    ]
    block = pl.BlockSpec((GROUP, height, width), lambda i: (i, 0, 0))
    long_y = height + 2 * RADIUS
    return pl.pallas_call(
        cone_kernel,
        grid=(steps,),
        in_specs=[block, packed, packed]
        + strip_specs * 2
        + [whole_spec(t.shape) for t in tables],
        out_specs=block,
        out_shape=jax.ShapeDtypeStruct(sens.shape, jnp.float32),
        compiler_params=params(),
        cost_estimate=cost(planes * 12 * long_y * 256 * (long_y + 256), 16 * sens.size),
        name="cone",
    )(sens, left, right, above, above, above, below, below, below, *tables)


def step_kernel(first, second, third, density, mask, *rest):
    out = rest[-1]
    planes, rows = out.shape[:2]
    length = RADIUS_Z + 1
    parts = (first, second, third)
    for start in range(0, rows, 8):
        at = slice(start, start + 8)

        def cell(z):
            return parts[z // planes][z % planes, at]

        box = cell(0)
        for z in range(1, length):
            box = box + cell(z)
        boxes = [box]
        for z in range(1, 2 * planes):
            box = box + (cell(z + length - 1) - cell(z - 1))
            boxes.append(box)
        tent = boxes[0]
        for z in range(1, length):
            tent = tent + boxes[z]
        for z in range(planes):
            if z > 0:
                tent = tent + (boxes[z + length - 1] - boxes[z - 1])
            moved = density[z, at] - (MOVE_STEP / float(length * length)) * tent
            moved = jnp.minimum(jnp.maximum(moved, 0.0), 1.0)
            out[z, at] = jnp.where(mask[z, at] == 1, 0.0, moved)


def density_step(first, second, third, density, mask, half, onto=None):
    planes, height, width = first.shape
    rows = 32
    block = pl.BlockSpec((planes, rows, width), lambda i: (0, i, 0))
    placed = pl.BlockSpec((planes, rows, width), lambda i: (half, i, 0))
    operands = [first, second, third, density, mask]
    in_specs = [block] * 3 + [placed] * 2
    aliases = {}
    if onto is not None:
        aliases[len(operands)] = 0
        operands.append(onto)
        in_specs.append(pl.BlockSpec(memory_space=pl.ANY))
    return pl.pallas_call(
        step_kernel,
        grid=(height // rows,),
        in_specs=in_specs,
        out_specs=placed,
        out_shape=jax.ShapeDtypeStruct(density.shape, jnp.float32),
        input_output_aliases=aliases,
        compiler_params=params(),
        cost_estimate=cost(12 * first.size, 24 * first.size),
        name="step",
    )(*operands)


def exchange(faces):
    xlo, xhi, ylo, yhi = faces
    return (
        to_next(xhi, "gx"),
        to_prev(xlo, "gx"),
        to_next(yhi, "gy"),
        to_prev(ylo, "gy"),
    )


def on_device(density, design_mask, velocity, adjoint_source, adjoint_start):
    depth, height, width = density.shape
    tables = cone_tables(height, width)
    blocks = depth // GROUP
    half = blocks // 2
    zlo = to_next(adjoint_start[:, depth - 1], "gz")
    zhi = to_prev(adjoint_start[:, 0], "gz")
    arrived = exchange(faces_of(adjoint_start))
    inner = sweep(
        adjoint_start, adjoint_source, density, arrived, 1, blocks - 2, faces=True
    )
    outer = sweep(
        adjoint_start, adjoint_source, density, arrived, 0, 2, blocks - 1,
        zlo=zlo, zhi=zhi, faces=True, held=inner[1:], onto=[(0, inner[0])],
    )
    once = outer[0]
    zlo = to_next(once[:, depth - 1], "gz")
    zhi = to_prev(once[:, 0], "gz")
    arrived = exchange(outer[1:])
    run = functools.partial(sweep, once, adjoint_source, density, arrived, velocity=velocity)
    inner = run(1, half - 1)
    adjoint, *low = run(0, 1, zlo=zlo, onto=list(enumerate(inner)))
    adjoint, *high = run(half, half, zhi=zhi, sens_base=half, onto=[(0, adjoint)])
    low = cone_filter(*low, tables)
    above = to_prev(low, "gz")
    high = cone_filter(*high, tables)
    below = to_next(high, "gz")
    moved = density_step(low, high, above, density, design_mask, 1)
    density_next = density_step(below, low, high, density, design_mask, 0, moved)
    return (density_next, adjoint)


def solution(mesh):
    return jax.shard_map(
        on_device,
        mesh=mesh,
        in_specs=(
            P("gz", "gy", "gx"),
            P("gz", "gy", "gx"),
            P(None, "gz", "gy", "gx"),
            P(None, "gz", "gy", "gx"),
            P(None, "gz", "gy", "gx"),
        ),
        out_specs=(P("gz", "gy", "gx"), P(None, "gz", "gy", "gx")),
        check_vma=False,
    )
```

time: 812 us -> 253 us (0.31)
  other arithmetic: 226 us -> 0.11 us
  local copies, waits for them, and re-layouts: 179 us -> 5.47 us
  matrix products: 162 us -> 0 us
  Pallas kernels: 0 us -> 139 us
  waiting for transfers between devices: 205 us -> 78.3 us
    dot_general x15 -> x0, matrix products: 162 us -> none  [the longest x4 47.6 us: along_y(): jnp.einsum('pbyk,byq->pqk', field, table, precision=HIGH, preferred_eleme...]
    pallas_call x0 -> x10, Pallas kernels: none -> 139 us  [the longest x5 60.4 us: sweep(): pl.pallas_call(functools.partial(sweep_kernel, conf), grid=(count,), in_s...]
    reduce_sum x2 -> x0, other arithmetic: 95.8 us -> none  [the longest x1 94.7 us: on_device(): jnp.sum(velocity.astype(jnp.float32) * adjoint, axis=0)]
    add x2 -> x0, other arithmetic: 95.7 us -> none  [the longest x1 88.7 us: jacobi_sweep(): return center + OMEGA * (source - (diagonal * center - beside)) / diagonal]
    all_to_all x2 -> x0, waiting for transfers between devices: 65.6 us -> none  [the longest x1 34.4 us: on_device(): lax.all_to_all(sending, ('gx', 'gy'), split_axis=0, concat_axis=2, tiled=...]
    slice x9 -> x6, local copies, waits for them, and re-layouts: 62.8 us -> 0.11 us  [cone_filter(): s[:, :RADIUS]]
    ppermute x14 -> x22, waiting for transfers between devices: 139 us -> 78.3 us  [the longest x11 46 us: to_next(): lax.ppermute(array, axis, [(i, (i + 1) % count) for i in range(count)])]
    unnamed x21 -> x30, local copies, waits for them, and re-layouts: 52.9 us -> 3.02 us
  transfers between devices with their start and end apart: 16 -> 22, of which waited for: 12 -> 9; matrix products, arithmetic and copies ran while one was open for 12% -> 0% of each run, Pallas kernels for 0% -> 49%
where the time goes in v1:
time: 253 us; the launch traced here: 252 us
  Pallas kernels  139 us (55%)
  waiting for transfers between devices  78.3 us (31%)
  starting transfers between devices  28.5 us (11%)
  local copies, waits for them, and re-layouts  5.47 us (2%)
    pallas_call x5, Pallas kernels, sweep(): pl.pallas_call(functools.partial(sweep_kernel, conf), grid=(count,), in_s...  60.4 us
    pallas_call x2, Pallas kernels, cone_filter(): pl.pallas_call(cone_kernel, grid=(steps,), in_specs=[block, packed, packe...  53.8 us
    ppermute x11, waiting for transfers between devices, to_next(): lax.ppermute(array, axis, [(i, (i + 1) % count) for i in range(count)])  46 us
    ppermute x11, waiting for transfers between devices, to_prev(): lax.ppermute(array, axis, [((i + 1) % count, i) for i in range(count)])  32.3 us
    ppermute x11, starting transfers between devices, to_prev(): lax.ppermute(array, axis, [((i + 1) % count, i) for i in range(count)])  21.9 us
    pallas_call x2, Pallas kernels, density_step(): pl.pallas_call(step_kernel, grid=(height // rows,), in_specs=in_specs, ou...  13.9 us
    pallas_call x1, Pallas kernels, faces_of(): pl.pallas_call(functools.partial(faces_kernel, depth), grid=(depth // GRO...  10.8 us
    ppermute x11, starting transfers between devices, to_next(): lax.ppermute(array, axis, [(i, (i + 1) % count) for i in range(count)])  6.54 us
  transfers between devices with their start and end apart: 22, of which 9 were waited for; matrix products, arithmetic and copies ran while one was open for 0% of the time, Pallas kernels for 49%

profile of v1, /device:TPU:0, one launch (start us, length us, event | category | flops | bytes accessed | tf_op | source)
XLA Modules:
  0.0 252.2 jit_solution(6680152058452182941)
XLA Ops:
  1.8 5.1 %collective-permute-start.5 = (f32[3,256,128]{2,1,0:T(8,128)S(1)}, f32[3,256,128]{2,1,0:T(8,128)S(1)}, u32[]{:S(2)}, u32[]{:S(2)}) collective-permute-start(f32[3,256,128]{2,1,0:T(8,128)S(1)} %get-tuple-element.56), channel_id=1, source_target_pairs={{1,0},{2,1},{3,2},{0,3},{5,4},{6,5},{7,6},{4,7},{9,8},{10,9},{11,1... | collective-permute-start | bytes 1179656 | tf_op jit(solution)/shard_map/ppermute | solution.py:42
  6.9 10.8 %faces.1 = (f32[256,128]{1,0:T(8,128)S(1)}, f32[256,128]{1,0:T(8,128)S(1)}, f32[96,128]{1,0:T(8,128)S(1)}, f32[96,128]{1,0:T(8,128)S(1)}) custom-call(f32[3,32,256,128]{3,2,1,0:T(8,128)} %refs_2_.3), custom_call_target="tpu_custom_call" | custom-call | flops 31457280 | bytes 12582912 | tf_op jit(solution)/shard_map/faces/pallas_call | solution.py:83
  17.8 1.7 collective-permute-start.1
  21.1 2.6 %collective-permute-done.2.refs_7_ = f32[96,128]{1,0:T(8,128)S(1)} collective-permute-done((f32[96,128]{1,0:T(8,128)S(1)}, f32[96,128]{1,0:T(8,128)S(1)}, u32[]{:S(2)}, u32[]{:S(2)}) %collective-permute-start.2) | collective-permute-done | bytes 49184 | tf_op jit(solution)/shard_map/ppermute | solution.py:37
  25.2 2.6 %collective-permute-done.3.refs_8_ = f32[96,128]{1,0:T(8,128)S(1)} collective-permute-done((f32[96,128]{1,0:T(8,128)S(1)}, f32[96,128]{1,0:T(8,128)S(1)}, u32[]{:S(2)}, u32[]{:S(2)}) %collective-permute-start.3) | collective-permute-done | bytes 49184 | tf_op jit(solution)/shard_map/ppermute | solution.py:42
  27.8 21.9 %sweep.5 = (f32[3,32,256,128]{3,2,1,0:T(8,128)}, f32[256,128]{1,0:T(8,128)S(1)}, f32[256,128]{1,0:T(8,128)S(1)}, f32[96,128]{1,0:T(8,128)S(1)}, f32[96,128]{1,0:T(8,128)S(1)}) custom-call(f32[3,32,256,128]{3,2,1,0:T(8,128)} %refs_2_.3, f32[3,32,256,128]{3,2,1,0:T(8,128)} %refs_2_.3, f32[3,32,256,128]{3,2,1,0:T(8,128)} %refs_2_.3, ...), custom_call_target="tpu_custom_call" | custom-call | flops 94371840 | bytes 33030144 | tf_op jit(solution)/shard_map/sweep/pallas_call | solution.py:266
  49.7 9.3 %sweep.6 = (f32[3,32,256,128]{3,2,1,0:T(8,128)}, f32[256,128]{1,0:T(8,128)S(1)}, f32[256,128]{1,0:T(8,128)S(1)}, f32[96,128]{1,0:T(8,128)S(1)}, f32[96,128]{1,0:T(8,128)S(1)}) custom-call(f32[3,32,256,128]{3,2,1,0:T(8,128)} %refs_2_.3, f32[3,32,256,128]{3,2,1,0:T(8,128)} %refs_2_.3, f32[3,32,256,128]{3,2,1,0:T(8,128)} %refs_2_.3, ...), custom_call_target="tpu_custom_call", output_to_operand_aliasing={{0}: (15, {})} | custom-call | flops 31457280 | bytes 11010048 | tf_op jit(solution)/shard_map/sweep/pallas_call | solution.py:266
  60.2 3.8 %collective-permute-start.10 = (f32[3,256,128]{2,1,0:T(8,128)S(1)}, f32[3,256,128]{2,1,0:T(8,128)S(1)}, u32[]{:S(2)}, u32[]{:S(2)}) collective-permute-start(f32[3,256,128]{2,1,0:T(8,128)S(1)} %get-tuple-element.55), channel_id=1, source_target_pairs={{1,0},{2,1},{3,2},{0,3},{5,4},{6,5},{7,6},{4,7},{9,8},{10,9},{11,1... | collective-permute-start | bytes 1179656 | tf_op jit(solution)/shard_map/ppermute | solution.py:42
  64.0 1.7 collective-permute-start.7
  67.3 2.6 %collective-permute-done.8.refs_7_ = f32[96,128]{1,0:T(8,128)S(1)} collective-permute-done((f32[96,128]{1,0:T(8,128)S(1)}, f32[96,128]{1,0:T(8,128)S(1)}, u32[]{:S(2)}, u32[]{:S(2)}) %collective-permute-start.8) | collective-permute-done | bytes 49184 | tf_op jit(solution)/shard_map/ppermute | solution.py:37
  71.4 2.6 %collective-permute-done.9.refs_8_ = f32[96,128]{1,0:T(8,128)S(1)} collective-permute-done((f32[96,128]{1,0:T(8,128)S(1)}, f32[96,128]{1,0:T(8,128)S(1)}, u32[]{:S(2)}, u32[]{:S(2)}) %collective-permute-start.9) | collective-permute-done | bytes 49184 | tf_op jit(solution)/shard_map/ppermute | solution.py:42
  74.0 10.6 %sweep.7 = (f32[3,32,256,128]{3,2,1,0:T(8,128)}, f32[16,256,128]{2,1,0:T(8,128)S(1)}, f32[4,256,128]{2,1,0:T(8,128)S(1)}, f32[4,256,128]{2,1,0:T(8,128)S(1)}) custom-call(f32[3,32,256,128]{3,2,1,0:T(8,128)} %get-tuple-element.37.refs_0_.refs_1_.refs_2_, f32[3,32,256,128]{3,2,1,0:T(8,128)} %get-tuple-element.37.refs_0_.refs_1_.refs_2_, ...), custom_call_target="tpu_custom_call" | custom-call | flops 47185920 | bytes 16515072 | tf_op jit(solution)/shard_map/sweep/pallas_call | solution.py:266
  84.6 5.5 %sweep.8 = (f32[3,32,256,128]{3,2,1,0:T(8,128)}, f32[16,256,128]{2,1,0:T(8,128)S(1)}, f32[4,256,128]{2,1,0:T(8,128)S(1)}, f32[4,256,128]{2,1,0:T(8,128)S(1)}) custom-call(f32[3,32,256,128]{3,2,1,0:T(8,128)} %get-tuple-element.37.refs_0_.refs_1_.refs_2_, ...), custom_call_target="tpu_custom_call", output_to_operand_aliasing={{0}: (11, {}), {1}: (12, {}), {2}: (13, {}), {3}: (14, {})} | custom-call | flops 15728640 | bytes 5505024 | tf_op jit(solution)/shard_map/sweep/pallas_call | solution.py:266
  90.1 1.7 collective-permute-start.18
  91.9 13.0 %sweep.9 = (f32[3,32,256,128]{3,2,1,0:T(8,128)}, f32[16,256,128]{2,1,0:T(8,128)S(1)}, f32[4,256,128]{2,1,0:T(8,128)S(1)}, f32[4,256,128]{2,1,0:T(8,128)S(1)}) custom-call(f32[3,32,256,128]{3,2,1,0:T(8,128)} %get-tuple-element.37.refs_0_.refs_1_.refs_2_, ...), custom_call_target="tpu_custom_call", output_to_operand_aliasing={{0}: (11, {})} | custom-call | flops 62914560 | bytes 22020096 | tf_op jit(solution)/shard_map/sweep/pallas_call | solution.py:266
  109.2 8.3 %collective-permute-done.12.left = f32[4,256,128]{2,1,0:T(8,128)S(1)} collective-permute-done((f32[4,256,128]{2,1,0:T(8,128)S(1)}, f32[4,256,128]{2,1,0:T(8,128)S(1)}, u32[]{:S(2)}, u32[]{:S(2)}) %collective-permute-start.12) | collective-permute-done | bytes 524320 | tf_op jit(solution)/shard_map/ppermute | solution.py:37
  120.6 6.9 %collective-permute-done.20.below.below_left.below_right = f32[24,32,128]{2,1,0:T(8,128)S(1)} collective-permute-done((f32[24,32,128]{2,1,0:T(8,128)S(1)}, f32[24,32,128]{2,1,0:T(8,128)S(1)}, u32[]{:S(2)}, u32[]{:S(2)}) %collective-permute-start.20) | collective-permute-done | bytes 393248 | tf_op jit(solution)/shard_map/ppermute | solution.py:42
  127.5 26.9 %cone.3.first.second = f32[16,256,128]{2,1,0:T(8,128)} custom-call(f32[16,256,128]{2,1,0:T(8,128)} %copy-done.3, f32[4,256,128]{2,1,0:T(8,128)S(1)} %collective-permute-done.17.left, f32[4,256,128]{2,1,0:T(8,128)S(1)} %collective-permute-done.18.right, f32[24,32,128]{2,1,0:T(8,128)S(1)} %collective-permute-done.19.above.above_left.above_right, ...), custom_call_target="tpu_custom_call" | custom-call | flops 9059696640 | bytes 8388608 | tf_op jit(solution)/shard_map/cone/pallas_call | solution.py:378
  154.4 1.9 collective-permute-start.21
  156.3 26.9 %cone.2.second.third = f32[16,256,128]{2,1,0:T(8,128)} custom-call(f32[16,256,128]{2,1,0:T(8,128)} %copy-done.4, f32[4,256,128]{2,1,0:T(8,128)S(1)} %collective-permute-done.12.left, f32[4,256,128]{2,1,0:T(8,128)S(1)} %collective-permute-done.13.right, f32[24,32,128]{2,1,0:T(8,128)S(1)} %collective-permute-done.14.above.above_left.above_right, ...), custom_call_target="tpu_custom_call" | custom-call | flops 9059696640 | bytes 8388608 | tf_op jit(solution)/shard_map/cone/pallas_call | solution.py:378
  183.4 19.4 %collective-permute-done.21.third = f32[16,256,128]{2,1,0:T(8,128)S(1)} collective-permute-done((f32[16,256,128]{2,1,0:T(8,128)}, f32[16,256,128]{2,1,0:T(8,128)S(1)}, u32[]{:S(2)}, u32[]{:S(2)}) %collective-permute-start.21) | collective-permute-done | bytes 2097184 | tf_op jit(solution)/shard_map/ppermute | solution.py:42
  205.7 7.0 %step.2.rest_0_ = f32[32,256,128]{2,1,0:T(8,128)} custom-call(f32[16,256,128]{2,1,0:T(8,128)S(1)} %copy-done.1, f32[16,256,128]{2,1,0:T(8,128)S(1)} %copy-done.2, f32[16,256,128]{2,1,0:T(8,128)} %copy-done.14, f32[32,256,128]{2,1,0:T(8,128)} %density.3, s32[32,256,128]{2,1,0:T(8,128)} %mask.3), custom_call_target="tpu_custom_call" | custom-call | flops 6291456 | bytes 12582912 | tf_op jit(solution)/shard_map/step/pallas_call | solution.py:433
  212.7 32.5 %collective-permute-done.16.first = f32[16,256,128]{2,1,0:T(8,128)S(1)} collective-permute-done((f32[16,256,128]{2,1,0:T(8,128)}, f32[16,256,128]{2,1,0:T(8,128)S(1)}, u32[]{:S(2)}, u32[]{:S(2)}) %collective-permute-start.16) | collective-permute-done | bytes 2097184 | tf_op jit(solution)/shard_map/ppermute | solution.py:37
  245.2 7.0 %step.3 = f32[32,256,128]{2,1,0:T(8,128)} custom-call(f32[16,256,128]{2,1,0:T(8,128)S(1)} %collective-permute-done.16.first, f32[16,256,128]{2,1,0:T(8,128)S(1)} %copy-done.1, f32[16,256,128]{2,1,0:T(8,128)} %cone.2.second.third, f32[32,256,128]{2,1,0:T(8,128)} %density.3, s32[32,256,128]{2,1,0:T(8,128)} %mask.3, ...), custom_call_target="tpu_custom_call", output_to_operand_aliasing={{}: (5, {})} | custom-call | flops 6291456 | bytes 12582912 | tf_op jit(solution)/shard_map/step/pallas_call | solution.py:433
  (72 shorter events, 18.9 us)
Async XLA Ops:
  1.8 47.9 %collective-permute-start.5 = (f32[3,256,128]{2,1,0:T(8,128)S(1)}, f32[3,256,128]{2,1,0:T(8,128)S(1)}, u32[]{:S(2)}, u32[]{:S(2)}) collective-permute-start(f32[3,256,128]{2,1,0:T(8,128)S(1)} %get-tuple-element.56), channel_id=1, source_target_pairs={{1,0},{2,1},{3,2},{0,3},{5,4},{6,5},{7,6},{4,7},{9,8},{10,9},{11,1... | collective-permute-start | bytes 1179656 | tf_op jit(solution)/shard_map/ppermute | solution.py:42
  6.9 42.8 %collective-permute-start.4 = (f32[3,256,128]{2,1,0:T(8,128)S(1)}, f32[3,256,128]{2,1,0:T(8,128)S(1)}, u32[]{:S(2)}, u32[]{:S(2)}) collective-permute-start(f32[3,256,128]{2,1,0:T(8,128)S(1)} %get-tuple-element.57), channel_id=1, source_target_pairs={{0,1},{1,2},{2,3},{3,0},{4,5},{5,6},{6,7},{7,4},{8,9},{9,10},{10,1... | collective-permute-start | bytes 1179656 | tf_op jit(solution)/shard_map/ppermute | solution.py:37
  17.8 10.0 %collective-permute-start = (f32[256,128]{1,0:T(8,128)S(1)}, f32[256,128]{1,0:T(8,128)S(1)}, u32[]{:S(2)}, u32[]{:S(2)}) collective-permute-start(f32[256,128]{1,0:T(8,128)S(1)} %get-tuple-element.28), channel_id=1, source_target_pairs={{0,8},{8,16},{16,24},{24,0},{1,9},{9,17},{17,25},{25,1},{2,10},{10... | collective-permute-start | bytes 393224 | tf_op jit(solution)/shard_map/ppermute | solution.py:37
  17.8 9.9 %collective-permute-start.1 = (f32[256,128]{1,0:T(8,128)S(1)}, f32[256,128]{1,0:T(8,128)S(1)}, u32[]{:S(2)}, u32[]{:S(2)}) collective-permute-start(f32[256,128]{1,0:T(8,128)S(1)} %get-tuple-element.29), channel_id=1, source_target_pairs={{8,0},{16,8},{24,16},{0,24},{9,1},{17,9},{25,17},{1,25},{10,2},{18... | collective-permute-start | bytes 393224 | tf_op jit(solution)/shard_map/ppermute | solution.py:42
  19.6 4.1 %collective-permute-start.2 = (f32[96,128]{1,0:T(8,128)S(1)}, f32[96,128]{1,0:T(8,128)S(1)}, u32[]{:S(2)}, u32[]{:S(2)}) collective-permute-start(f32[96,128]{1,0:T(8,128)S(1)} %get-tuple-element.30), channel_id=1, source_target_pairs={{0,4},{4,0},{1,5},{5,1},{2,6},{6,2},{3,7},{7,3},{8,12},{12,8},{9,1... | collective-permute-start | bytes 147464 | tf_op jit(solution)/shard_map/ppermute | solution.py:37
  23.7 4.1 %collective-permute-start.3 = (f32[96,128]{1,0:T(8,128)S(1)}, f32[96,128]{1,0:T(8,128)S(1)}, u32[]{:S(2)}, u32[]{:S(2)}) collective-permute-start(f32[96,128]{1,0:T(8,128)S(1)} %get-tuple-element.31), channel_id=1, source_target_pairs={{4,0},{0,4},{5,1},{1,5},{6,2},{2,6},{7,3},{3,7},{12,8},{8,12},{13,... | collective-permute-start | bytes 147464 | tf_op jit(solution)/shard_map/ppermute | solution.py:42
  60.2 24.4 %collective-permute-start.11 = (f32[3,256,128]{2,1,0:T(8,128)S(1)}, f32[3,256,128]{2,1,0:T(8,128)S(1)}, u32[]{:S(2)}, u32[]{:S(2)}) collective-permute-start(f32[3,256,128]{2,1,0:T(8,128)S(1)} %get-tuple-element.54), channel_id=1, source_target_pairs={{0,1},{1,2},{2,3},{3,0},{4,5},{5,6},{6,7},{7,4},{8,9},{9,10},{10,1... | collective-permute-start | bytes 1179656 | tf_op jit(solution)/shard_map/ppermute | solution.py:37
  60.2 31.6 %collective-permute-start.10 = (f32[3,256,128]{2,1,0:T(8,128)S(1)}, f32[3,256,128]{2,1,0:T(8,128)S(1)}, u32[]{:S(2)}, u32[]{:S(2)}) collective-permute-start(f32[3,256,128]{2,1,0:T(8,128)S(1)} %get-tuple-element.55), channel_id=1, source_target_pairs={{1,0},{2,1},{3,2},{0,3},{5,4},{6,5},{7,6},{4,7},{9,8},{10,9},{11,1... | collective-permute-start | bytes 1179656 | tf_op jit(solution)/shard_map/ppermute | solution.py:42
  64.0 9.9 %collective-permute-start.6 = (f32[256,128]{1,0:T(8,128)S(1)}, f32[256,128]{1,0:T(8,128)S(1)}, u32[]{:S(2)}, u32[]{:S(2)}) collective-permute-start(f32[256,128]{1,0:T(8,128)S(1)} %get-tuple-element.38), channel_id=1, source_target_pairs={{0,8},{8,16},{16,24},{24,0},{1,9},{9,17},{17,25},{25,1},{2,10},{10... | collective-permute-start | bytes 393224 | tf_op jit(solution)/shard_map/ppermute | solution.py:37
  64.0 9.9 %collective-permute-start.7 = (f32[256,128]{1,0:T(8,128)S(1)}, f32[256,128]{1,0:T(8,128)S(1)}, u32[]{:S(2)}, u32[]{:S(2)}) collective-permute-start(f32[256,128]{1,0:T(8,128)S(1)} %get-tuple-element.39), channel_id=1, source_target_pairs={{8,0},{16,8},{24,16},{0,24},{9,1},{17,9},{25,17},{1,25},{10,2},{18... | collective-permute-start | bytes 393224 | tf_op jit(solution)/shard_map/ppermute | solution.py:42
  65.8 4.1 %collective-permute-start.8 = (f32[96,128]{1,0:T(8,128)S(1)}, f32[96,128]{1,0:T(8,128)S(1)}, u32[]{:S(2)}, u32[]{:S(2)}) collective-permute-start(f32[96,128]{1,0:T(8,128)S(1)} %get-tuple-element.40), channel_id=1, source_target_pairs={{0,4},{4,0},{1,5},{5,1},{2,6},{6,2},{3,7},{7,3},{8,12},{12,8},{9,1... | collective-permute-start | bytes 147464 | tf_op jit(solution)/shard_map/ppermute | solution.py:37
  69.9 4.1 %collective-permute-start.9 = (f32[96,128]{1,0:T(8,128)S(1)}, f32[96,128]{1,0:T(8,128)S(1)}, u32[]{:S(2)}, u32[]{:S(2)}) collective-permute-start(f32[96,128]{1,0:T(8,128)S(1)} %get-tuple-element.41), channel_id=1, source_target_pairs={{4,0},{0,4},{5,1},{1,5},{6,2},{2,6},{7,3},{3,7},{12,8},{8,12},{13,... | collective-permute-start | bytes 147464 | tf_op jit(solution)/shard_map/ppermute | solution.py:42
  90.1 16.8 %collective-permute-start.17 = (f32[4,256,128]{2,1,0:T(8,128)S(1)}, f32[4,256,128]{2,1,0:T(8,128)S(1)}, u32[]{:S(2)}, u32[]{:S(2)}) collective-permute-start(f32[4,256,128]{2,1,0:T(8,128)S(1)} %get-tuple-element.51), channel_id=1, source_target_pairs={{0,8},{8,16},{16,24},{24,0},{1,9},{9,17},{17,25},{25,1},{2,10},{10... | collective-permute-start | bytes 1572872 | tf_op jit(solution)/shard_map/ppermute | solution.py:37
  90.1 16.8 %collective-permute-start.18 = (f32[4,256,128]{2,1,0:T(8,128)S(1)}, f32[4,256,128]{2,1,0:T(8,128)S(1)}, u32[]{:S(2)}, u32[]{:S(2)}) collective-permute-start(f32[4,256,128]{2,1,0:T(8,128)S(1)} %get-tuple-element.52), channel_id=1, source_target_pairs={{8,0},{16,8},{24,16},{0,24},{9,1},{17,9},{25,17},{1,25},{10,2},{18... | collective-permute-start | bytes 1572872 | tf_op jit(solution)/shard_map/ppermute | solution.py:42
  104.9 49.6 %copy-start.4 = (f32[16,256,128]{2,1,0:T(8,128)}, f32[16,256,128]{2,1,0:T(8,128)S(1)}, u32[]{:S(2)}) copy-start(f32[16,256,128]{2,1,0:T(8,128)S(1)} %get-tuple-element.47.own) | copy-start | bytes 6291460
  105.0 12.4 %collective-permute-start.12 = (f32[4,256,128]{2,1,0:T(8,128)S(1)}, f32[4,256,128]{2,1,0:T(8,128)S(1)}, u32[]{:S(2)}, u32[]{:S(2)}) collective-permute-start(f32[4,256,128]{2,1,0:T(8,128)S(1)} %get-tuple-element.48), channel_id=1, source_target_pairs={{0,8},{8,16},{16,24},{24,0},{1,9},{9,17},{17,25},{25,1},{2,10},{10... | collective-permute-start | bytes 1572872 | tf_op jit(solution)/shard_map/ppermute | solution.py:37
  105.1 13.2 %collective-permute-start.13 = (f32[4,256,128]{2,1,0:T(8,128)S(1)}, f32[4,256,128]{2,1,0:T(8,128)S(1)}, u32[]{:S(2)}, u32[]{:S(2)}) collective-permute-start(f32[4,256,128]{2,1,0:T(8,128)S(1)} %get-tuple-element.49), channel_id=1, source_target_pairs={{8,0},{16,8},{24,16},{0,24},{9,1},{17,9},{25,17},{1,25},{10,2},{18... | collective-permute-start | bytes 1572872 | tf_op jit(solution)/shard_map/ppermute | solution.py:42
  107.0 13.6 %collective-permute-start.19 = (f32[24,32,128]{2,1,0:T(8,128)S(1)}, f32[24,32,128]{2,1,0:T(8,128)S(1)}, u32[]{:S(2)}, u32[]{:S(2)}) collective-permute-start(f32[24,32,128]{2,1,0:T(8,128)S(1)} %pad_maximum_fusion.2), channel_id=1, source_target_pairs={{0,4},{4,0},{1,5},{5,1},{2,6},{6,2},{3,7},{7,3},{8,12},{12,8},{9,1... | collective-permute-start | bytes 1179656 | tf_op jit(solution)/shard_map/ppermute | solution.py:37
  108.6 18.9 %collective-permute-start.20 = (f32[24,32,128]{2,1,0:T(8,128)S(1)}, f32[24,32,128]{2,1,0:T(8,128)S(1)}, u32[]{:S(2)}, u32[]{:S(2)}) collective-permute-start(f32[24,32,128]{2,1,0:T(8,128)S(1)} %pad_maximum_fusion.3), channel_id=1, source_target_pairs={{4,0},{0,4},{5,1},{1,5},{6,2},{2,6},{7,3},{3,7},{12,8},{8,12},{13,... | collective-permute-start | bytes 1179656 | tf_op jit(solution)/shard_map/ppermute | solution.py:42
  118.4 38.0 %collective-permute-start.14 = (f32[24,32,128]{2,1,0:T(8,128)S(1)}, f32[24,32,128]{2,1,0:T(8,128)S(1)}, u32[]{:S(2)}, u32[]{:S(2)}) collective-permute-start(f32[24,32,128]{2,1,0:T(8,128)S(1)} %pad_maximum_fusion), channel_id=1, source_target_pairs={{0,4},{4,0},{1,5},{5,1},{2,6},{6,2},{3,7},{7,3},{8,12},{12,8},{9,1... | collective-permute-start | bytes 1179656 | tf_op jit(solution)/shard_map/ppermute | solution.py:37
  120.0 36.3 %collective-permute-start.15 = (f32[24,32,128]{2,1,0:T(8,128)S(1)}, f32[24,32,128]{2,1,0:T(8,128)S(1)}, u32[]{:S(2)}, u32[]{:S(2)}) collective-permute-start(f32[24,32,128]{2,1,0:T(8,128)S(1)} %pad_maximum_fusion.1), channel_id=1, source_target_pairs={{4,0},{0,4},{5,1},{1,5},{6,2},{2,6},{7,3},{3,7},{12,8},{8,12},{13,... | collective-permute-start | bytes 1179656 | tf_op jit(solution)/shard_map/ppermute | solution.py:42
  154.4 49.7 %copy-start.1 = (f32[16,256,128]{2,1,0:T(8,128)S(1)}, f32[16,256,128]{2,1,0:T(8,128)}, u32[]{:S(2)}) copy-start(f32[16,256,128]{2,1,0:T(8,128)} %cone.3.first.second) | copy-start | bytes 6291460
  154.4 48.3 %collective-permute-start.21 = (f32[16,256,128]{2,1,0:T(8,128)}, f32[16,256,128]{2,1,0:T(8,128)S(1)}, u32[]{:S(2)}, u32[]{:S(2)}) collective-permute-start(f32[16,256,128]{2,1,0:T(8,128)} %cone.3.first.second), channel_id=1, source_target_pairs={{1,0},{2,1},{3,2},{0,3},{5,4},{6,5},{7,6},{4,7},{9,8},{10,9},{11,1... | collective-permute-start | bytes 6291464 | tf_op jit(solution)/shard_map/ppermute | solution.py:42
  183.2 62.0 %collective-permute-start.16 = (f32[16,256,128]{2,1,0:T(8,128)}, f32[16,256,128]{2,1,0:T(8,128)S(1)}, u32[]{:S(2)}, u32[]{:S(2)}) collective-permute-start(f32[16,256,128]{2,1,0:T(8,128)} %cone.2.second.third), channel_id=1, source_target_pairs={{0,1},{1,2},{2,3},{3,0},{4,5},{5,6},{6,7},{7,4},{8,9},{9,10},{10,1... | collective-permute-start | bytes 6291464 | tf_op jit(solution)/shard_map/ppermute | solution.py:37
  (13 other events, 243.5 us)

commit v2 on v1

--- a/solution.py
+++ b/solution.py
@@ -40,6 +40,14 @@
 def to_prev(array, axis):
     count = lax.axis_size(axis)
     return lax.ppermute(array, axis, [((i + 1) % count, i) for i in range(count)])
+
+
+def across_y(first_rows, last_rows):
+    if lax.axis_size("gy") == 2:
+        count = last_rows.shape[0]
+        arrived = to_next(jnp.concatenate([last_rows, first_rows], axis=0), "gy")
+        return arrived[:count], arrived[count:]
+    return to_next(last_rows, "gy"), to_prev(first_rows, "gy")
 
 
 def pack_faces(plane, lane, column, xlo, xhi, ylo, yhi):
@@ -90,6 +98,40 @@
         cost_estimate=cost(10 * adjoint.size, 4 * adjoint.size),
         name="faces",
     )(adjoint)
+
+
+def pack_edges(value, lane, j, pack_lo, pack_hi):
+    turned = pltpu.roll(value, RADIUS * (j + 1) % LANES, 1)
+    group = lane // RADIUS
+    low = jnp.where(group == (j + 1) % GROUP, turned, 0.0)
+    high = jnp.where(group == j, turned, 0.0)
+    if j == 0:
+        pack_lo[0] = low
+        pack_hi[0] = high
+    else:
+        pack_lo[0] += low
+        pack_hi[0] += high
+
+
+def edges_kernel(cells, pack_lo, pack_hi):
+    lane = lax.broadcasted_iota(jnp.int32, cells.shape[1:], 1)
+    for j in range(GROUP):
+        pack_edges(cells[j], lane, j, pack_lo, pack_hi)
+
+
+def edges_of(cells):
+    planes, height, width = cells.shape
+    packed = pl.BlockSpec((1, height, LANES), lambda i: (i, 0, 0))
+    return pl.pallas_call(
+        edges_kernel,
+        grid=(planes // GROUP,),
+        in_specs=[pl.BlockSpec((GROUP, height, width), lambda i: (i, 0, 0))],
+        out_specs=[packed] * 2,
+        out_shape=[jax.ShapeDtypeStruct((planes // GROUP, height, LANES), jnp.float32)] * 2,
+        compiler_params=params(),
+        cost_estimate=cost(4 * cells.size, 6 * cells.size),
+        name="edges",
+    )(cells)
 
 
 def sweep_kernel(conf, *refs):
@@ -178,16 +220,7 @@
             near = 1.0 / (1.0 + dens)
             value = (-2.0 * ALPHA_MAX) * near * near * total
             sens_out[j] = value
-            turned = pltpu.roll(value, RADIUS * (j + 1) % LANES, 1)
-            group = lane // RADIUS
-            low = jnp.where(group == (j + 1) % GROUP, turned, 0.0)
-            high = jnp.where(group == j, turned, 0.0)
-            if j == 0:
-                pack_lo[0] = low
-                pack_hi[0] = high
-            else:
-                pack_lo[0] += low
-                pack_hi[0] += high
+            pack_edges(value, lane, j, pack_lo, pack_hi)
 
 
 class Conf(tuple):
@@ -276,10 +309,10 @@
     )(*operands)
 
 
-def parts_of(table):
+def parts_of(table, axis):
     high = table.astype(ml_dtypes.bfloat16)
     low = (table - high.astype(np.float64)).astype(ml_dtypes.bfloat16)
-    return jnp.asarray(high), jnp.asarray(low)
+    return jnp.asarray(np.concatenate([high, high, low], axis=axis))
 
 
 def real_dft(length):
@@ -311,31 +344,29 @@
         right = width + RADIUS * ((j + 1) % GROUP)
         into_x[j, right : right + RADIUS] = basis_x[:, RADIUS + width : 2 * RADIUS + width].T
     tables = [
-        *parts_of(into_x),
-        *parts_of(basis_y),
-        *parts_of(basis_y[:, RADIUS : RADIUS + height].T),
-        *parts_of(basis_x[:, RADIUS : RADIUS + width]),
+        parts_of(into_x, 1),
+        parts_of(basis_y, 1),
+        parts_of(basis_y[:, RADIUS : RADIUS + height].T, 1),
+        parts_of(basis_x[:, RADIUS : RADIUS + width], 0),
         jnp.asarray(spectrum),
     ]
     return tables
 
 
-def split(value):
+def triple(value, axis):
     high = value.astype(jnp.bfloat16)
-    return high, (value - high.astype(jnp.float32)).astype(jnp.bfloat16)
-
-
-def product(left, right):
-    dot = functools.partial(jnp.dot, preferred_element_type=jnp.float32)
-    return dot(left[0], right[0]) + (dot(left[0], right[1]) + dot(left[1], right[0]))
+    low = (value - high.astype(jnp.float32)).astype(jnp.bfloat16)
+    return jnp.concatenate([high, low, high], axis=axis)
+
+
+dot = functools.partial(jnp.dot, preferred_element_type=jnp.float32)
 
 
 def cone_kernel(
     own, left, right,
     above, above_left, above_right,
     below, below_left, below_right,
-    into_high, into_low, y_high, y_low, yback_high, yback_low, xback_high, xback_low,
-    spectrum, out,
+    into_x, into_y, from_y, from_x, spectrum, out,
 ):
     for j in range(GROUP):
 
@@ -351,54 +382,67 @@
             ],
             axis=0,
         )
-        waves = product(split(cells), (into_high[j], into_low[j]))
-        waves = product((y_high[...], y_low[...]), split(waves)) * spectrum[...]
-        rows = product((yback_high[...], yback_low[...]), split(waves))
-        out[j] = product(split(rows), (xback_high[...], xback_low[...]))
-
-
-def cone_filter(sens, pack_lo, pack_hi, tables):
+        waves = dot(triple(cells, 1), into_x[j])
+        waves = dot(into_y[...], triple(waves, 0)) * spectrum[...]
+        rows = dot(from_y[...], triple(waves, 0))
+        out[j] = dot(triple(rows, 1), from_x[...])
+
+
+def cone_filter(sens, pack_lo, pack_hi, tables, parts=1):
     planes, height, width = sens.shape
     steps = planes // GROUP
     left = to_next(pack_hi, "gx")
     right = to_prev(pack_lo, "gx")
-    strips = [sens, left, right]
-    above = to_next(
-        jnp.concatenate([s[:, height - RADIUS :] for s in strips], axis=0), "gy"
-    )
-    below = to_prev(jnp.concatenate([s[:, :RADIUS] for s in strips], axis=0), "gy")
-    packed = pl.BlockSpec((1, height, LANES), lambda i: (i, 0, 0))
-    strip_specs = [
-        pl.BlockSpec((GROUP, RADIUS, width), lambda i: (i, 0, 0)),
-        pl.BlockSpec((1, RADIUS, LANES), lambda i: (planes + i, 0, 0)),
-        pl.BlockSpec((1, RADIUS, LANES), lambda i: (planes + steps + i, 0, 0)),
-    ]
-    block = pl.BlockSpec((GROUP, height, width), lambda i: (i, 0, 0))
+    above, below = across_y(sens[:, :RADIUS], sens[:, height - RADIUS :])
+    sides = jnp.concatenate([left[:, :RADIUS], right[:, :RADIUS]], axis=0)
+    far_sides = jnp.concatenate(
+        [left[:, height - RADIUS :], right[:, height - RADIUS :]], axis=0
+    )
+    above_sides, below_sides = across_y(sides, far_sides)
+    each = steps // parts
     long_y = height + 2 * RADIUS
-    return pl.pallas_call(
-        cone_kernel,
-        grid=(steps,),
-        in_specs=[block, packed, packed]
-        + strip_specs * 2
-        + [whole_spec(t.shape) for t in tables],
-        out_specs=block,
-        out_shape=jax.ShapeDtypeStruct(sens.shape, jnp.float32),
-        compiler_params=params(),
-        cost_estimate=cost(planes * 12 * long_y * 256 * (long_y + 256), 16 * sens.size),
-        name="cone",
-    )(sens, left, right, above, above, above, below, below, below, *tables)
-
-
-def step_kernel(first, second, third, density, mask, *rest):
-    out = rest[-1]
+
+    def part(base):
+        packed = pl.BlockSpec((1, height, LANES), lambda i: (base + i, 0, 0))
+        strip_specs = [
+            pl.BlockSpec((GROUP, RADIUS, width), lambda i: (base + i, 0, 0)),
+            pl.BlockSpec((1, RADIUS, LANES), lambda i: (base + i, 0, 0)),
+            pl.BlockSpec((1, RADIUS, LANES), lambda i: (steps + base + i, 0, 0)),
+        ]
+        block = pl.BlockSpec((GROUP, height, width), lambda i: (base + i, 0, 0))
+        return pl.pallas_call(
+            cone_kernel,
+            grid=(each,),
+            in_specs=[block, packed, packed]
+            + strip_specs * 2
+            + [whole_spec(t.shape) for t in tables],
+            out_specs=pl.BlockSpec((GROUP, height, width), lambda i: (i, 0, 0)),
+            out_shape=jax.ShapeDtypeStruct((each * GROUP, height, width), jnp.float32),
+            compiler_params=params(),
+            cost_estimate=cost(
+                each * GROUP * 24 * long_y * 256 * (long_y + 256), 16 * sens.size // parts
+            ),
+            name="cone",
+        )(
+            sens, left, right,
+            above, above_sides, above_sides, below, below_sides, below_sides,
+            *tables,
+        )
+
+    return [part(at * each) for at in range(parts)]
+
+
+def step_kernel(count, *refs):
+    density, mask, out = refs[count], refs[count + 1], refs[-1]
+    cells = [(part, z) for part in refs[:count] for z in range(part.shape[0])]
     planes, rows = out.shape[:2]
     length = RADIUS_Z + 1
-    parts = (first, second, third)
     for start in range(0, rows, 8):
         at = slice(start, start + 8)
 
         def cell(z):
-            return parts[z // planes][z % planes, at]
+            part, own = cells[z]
+            return part[own, at]
 
         box = cell(0)
         for z in range(1, length):
@@ -418,27 +462,29 @@
             out[z, at] = jnp.where(mask[z, at] == 1, 0.0, moved)
 
 
-def density_step(first, second, third, density, mask, half, onto=None):
-    planes, height, width = first.shape
+def density_step(parts, density, mask, half, onto=None):
+    depth, height, width = density.shape
+    planes = depth // 2
+    size = planes * height * width
     rows = 32
-    block = pl.BlockSpec((planes, rows, width), lambda i: (0, i, 0))
+    blocks = [pl.BlockSpec((p.shape[0], rows, width), lambda i: (0, i, 0)) for p in parts]
     placed = pl.BlockSpec((planes, rows, width), lambda i: (half, i, 0))
-    operands = [first, second, third, density, mask]
-    in_specs = [block] * 3 + [placed] * 2
+    operands = [*parts, density, mask]
+    in_specs = blocks + [placed] * 2
     aliases = {}
     if onto is not None:
         aliases[len(operands)] = 0
         operands.append(onto)
         in_specs.append(pl.BlockSpec(memory_space=pl.ANY))
     return pl.pallas_call(
-        step_kernel,
+        functools.partial(step_kernel, len(parts)),
         grid=(height // rows,),
         in_specs=in_specs,
         out_specs=placed,
         out_shape=jax.ShapeDtypeStruct(density.shape, jnp.float32),
         input_output_aliases=aliases,
         compiler_params=params(),
-        cost_estimate=cost(12 * first.size, 24 * first.size),
+        cost_estimate=cost(12 * size, 24 * size),
         name="step",
     )(*operands)
 
@@ -448,8 +494,7 @@
     return (
         to_next(xhi, "gx"),
         to_prev(xlo, "gx"),
-        to_next(yhi, "gy"),
-        to_prev(ylo, "gy"),
+        *across_y(ylo, yhi),
     )
 
 
@@ -476,12 +521,13 @@
     inner = run(1, half - 1)
     adjoint, *low = run(0, 1, zlo=zlo, onto=list(enumerate(inner)))
     adjoint, *high = run(half, half, zhi=zhi, sens_base=half, onto=[(0, adjoint)])
+    rim = to_prev(low[0], "gz")
     low = cone_filter(*low, tables)
-    above = to_prev(low, "gz")
-    high = cone_filter(*high, tables)
-    below = to_next(high, "gz")
-    moved = density_step(low, high, above, density, design_mask, 1)
-    density_next = density_step(below, low, high, density, design_mask, 0, moved)
+    high = cone_filter(*high, tables, parts=2)
+    below = [to_next(part, "gz") for part in high]
+    above = cone_filter(rim, *edges_of(rim), tables)
+    moved = density_step([*low, *high, *above], density, design_mask, 1)
+    density_next = density_step([*below, *low, *high], density, design_mask, 0, moved)
     return (density_next, adjoint)
 
 

time: 253 us -> 225 us (0.89)
  waiting for transfers between devices: 78.3 us -> 39.3 us
  Pallas kernels: 139 us -> 148 us
  starting transfers between devices: 28.5 us -> 31.2 us
  local copies, waits for them, and re-layouts: 5.47 us -> 2.78 us
    ppermute x11 -> x8, waiting for transfers between devices: 32.3 us -> 11.4 us  [to_prev(): lax.ppermute(array, axis, [((i + 1) % count, i) for i in range(count)])]
    ppermute x11 -> x17, waiting for transfers between devices: 46 us -> 27.9 us  [to_next(): lax.ppermute(array, axis, [(i, (i + 1) % count) for i in range(count)])]
    pallas_call x4 -> x7, Pallas kernels: 67.7 us -> 76.3 us  [the longest x4 61.6 us: part(): pl.pallas_call(cone_kernel, grid=(each,), in_specs=[block, packed, packed...]
    ppermute x11 -> x17, starting transfers between devices: 6.54 us -> 13 us  [to_next(): lax.ppermute(array, axis, [(i, (i + 1) % count) for i in range(count)])]
    ppermute x11 -> x8, starting transfers between devices: 21.9 us -> 18.2 us  [to_prev(): lax.ppermute(array, axis, [((i + 1) % count, i) for i in range(count)])]
    unnamed x30 -> x36, local copies, waits for them, and re-layouts: 3.02 us -> 0.1 us
  transfers between devices with their start and end apart: 22 -> 25, of which waited for: 9 -> 12; matrix products, arithmetic and copies ran while one was open for 0% -> 0% of each run, Pallas kernels for 49% -> 53%
where the time goes in v2:
time: 225 us; the launch traced here: 223 us
  Pallas kernels  148 us (66%)
  waiting for transfers between devices  39.3 us (17%)
  starting transfers between devices  31.2 us (14%)
  local copies, waits for them, and re-layouts  2.78 us (1%)
    pallas_call x4, Pallas kernels, part(): pl.pallas_call(cone_kernel, grid=(each,), in_specs=[block, packed, packed...  61.6 us
    pallas_call x5, Pallas kernels, sweep(): pl.pallas_call(functools.partial(sweep_kernel, conf), grid=(count,), in_s...  61 us
    ppermute x17, waiting for transfers between devices, to_next(): lax.ppermute(array, axis, [(i, (i + 1) % count) for i in range(count)])  27.9 us
    ppermute x8, starting transfers between devices, to_prev(): lax.ppermute(array, axis, [((i + 1) % count, i) for i in range(count)])  18.2 us
    pallas_call x2, Pallas kernels, density_step(): pl.pallas_call(functools.partial(step_kernel, len(parts)), grid=(height /...  13.9 us
    ppermute x17, starting transfers between devices, to_next(): lax.ppermute(array, axis, [(i, (i + 1) % count) for i in range(count)])  13 us
    ppermute x8, waiting for transfers between devices, to_prev(): lax.ppermute(array, axis, [((i + 1) % count, i) for i in range(count)])  11.4 us
    pallas_call x1, Pallas kernels, faces_of(): pl.pallas_call(functools.partial(faces_kernel, depth), grid=(depth // GRO...  10.8 us
  transfers between devices with their start and end apart: 25, of which 12 were waited for; matrix products, arithmetic and copies ran while one was open for 0% of the time, Pallas kernels for 53%

profile of v2, /device:TPU:0, one launch (start us, length us, event | category | flops | bytes accessed | tf_op | source)
XLA Modules:
  0.0 222.8 jit_solution(16649050742815422659)
XLA Ops:
  1.8 5.1 %collective-permute-start.4 = (f32[3,256,128]{2,1,0:T(8,128)S(1)}, f32[3,256,128]{2,1,0:T(8,128)S(1)}, u32[]{:S(2)}, u32[]{:S(2)}) collective-permute-start(f32[3,256,128]{2,1,0:T(8,128)S(1)} %get-tuple-element.60), channel_id=1, source_target_pairs={{1,0},{2,1},{3,2},{0,3},{5,4},{6,5},{7,6},{4,7},{9,8},{10,9},{11,1... | collective-permute-start | bytes 1179656 | tf_op jit(solution)/shard_map/ppermute | solution.py:42
  6.9 10.8 %faces.1 = (f32[256,128]{1,0:T(8,128)S(1)}, f32[256,128]{1,0:T(8,128)S(1)}, f32[96,128]{1,0:T(8,128)S(1)}, f32[96,128]{1,0:T(8,128)S(1)}) custom-call(f32[3,32,256,128]{3,2,1,0:T(8,128)} %refs_2_.3), custom_call_target="tpu_custom_call" | custom-call | flops 31457280 | bytes 12582912 | tf_op jit(solution)/shard_map/faces/pallas_call | solution.py:91
  24.2 21.9 %sweep.5 = (f32[3,32,256,128]{3,2,1,0:T(8,128)}, f32[256,128]{1,0:T(8,128)S(1)}, f32[256,128]{1,0:T(8,128)S(1)}, f32[96,128]{1,0:T(8,128)S(1)}, f32[96,128]{1,0:T(8,128)S(1)}) custom-call(f32[3,32,256,128]{3,2,1,0:T(8,128)} %refs_2_.3, f32[3,32,256,128]{3,2,1,0:T(8,128)} %refs_2_.3, f32[3,32,256,128]{3,2,1,0:T(8,128)} %refs_2_.3, ...), custom_call_target="tpu_custom_call" | custom-call | flops 94371840 | bytes 33030144 | tf_op jit(solution)/shard_map/sweep/pallas_call | solution.py:299
  46.0 9.3 %sweep.6 = (f32[3,32,256,128]{3,2,1,0:T(8,128)}, f32[256,128]{1,0:T(8,128)S(1)}, f32[256,128]{1,0:T(8,128)S(1)}, f32[96,128]{1,0:T(8,128)S(1)}, f32[96,128]{1,0:T(8,128)S(1)}) custom-call(f32[3,32,256,128]{3,2,1,0:T(8,128)} %refs_2_.3, f32[3,32,256,128]{3,2,1,0:T(8,128)} %refs_2_.3, f32[3,32,256,128]{3,2,1,0:T(8,128)} %refs_2_.3, ...), custom_call_target="tpu_custom_call", output_to_operand_aliasing={{0}: (15, {})} | custom-call | flops 31457280 | bytes 11010048 | tf_op jit(solution)/shard_map/sweep/pallas_call | solution.py:299
  56.6 3.8 %collective-permute-start.8 = (f32[3,256,128]{2,1,0:T(8,128)S(1)}, f32[3,256,128]{2,1,0:T(8,128)S(1)}, u32[]{:S(2)}, u32[]{:S(2)}) collective-permute-start(f32[3,256,128]{2,1,0:T(8,128)S(1)} %get-tuple-element.59), channel_id=1, source_target_pairs={{1,0},{2,1},{3,2},{0,3},{5,4},{6,5},{7,6},{4,7},{9,8},{10,9},{11,1... | collective-permute-start | bytes 1179656 | tf_op jit(solution)/shard_map/ppermute | solution.py:42
  62.7 3.3 %collective-permute-done.7 = f32[192,128]{1,0:T(8,128)S(1)} collective-permute-done((f32[192,128]{1,0:T(8,128)S(1)}, f32[192,128]{1,0:T(8,128)S(1)}, u32[]{:S(2)}, u32[]{:S(2)}) %collective-permute-start.7) | collective-permute-done | bytes 98336 | tf_op jit(solution)/shard_map/ppermute | solution.py:37
  66.0 10.6 %sweep.7 = (f32[3,32,256,128]{3,2,1,0:T(8,128)}, f32[16,256,128]{2,1,0:T(8,128)S(1)}, f32[4,256,128]{2,1,0:T(8,128)S(1)}, f32[4,256,128]{2,1,0:T(8,128)S(1)}) custom-call(f32[3,32,256,128]{3,2,1,0:T(8,128)} %get-tuple-element.39.refs_0_.refs_1_.refs_2_, f32[3,32,256,128]{3,2,1,0:T(8,128)} %get-tuple-element.39.refs_0_.refs_1_.refs_2_, ...), custom_call_target="tpu_custom_call" | custom-call | flops 47185920 | bytes 16515072 | tf_op jit(solution)/shard_map/sweep/pallas_call | solution.py:299
  76.6 5.5 %sweep.8 = (f32[3,32,256,128]{3,2,1,0:T(8,128)}, f32[16,256,128]{2,1,0:T(8,128)S(1)}, f32[4,256,128]{2,1,0:T(8,128)S(1)}, f32[4,256,128]{2,1,0:T(8,128)S(1)}) custom-call(f32[3,32,256,128]{3,2,1,0:T(8,128)} %get-tuple-element.39.refs_0_.refs_1_.refs_2_, ...), custom_call_target="tpu_custom_call", output_to_operand_aliasing={{0}: (11, {}), {1}: (12, {}), {2}: (13, {}), {3}: (14, {})} | custom-call | flops 15728640 | bytes 5505024 | tf_op jit(solution)/shard_map/sweep/pallas_call | solution.py:299
  82.2 13.8 %sweep.9 = (f32[3,32,256,128]{3,2,1,0:T(8,128)}, f32[16,256,128]{2,1,0:T(8,128)S(1)}, f32[4,256,128]{2,1,0:T(8,128)S(1)}, f32[4,256,128]{2,1,0:T(8,128)S(1)}) custom-call(f32[3,32,256,128]{3,2,1,0:T(8,128)} %get-tuple-element.39.refs_0_.refs_1_.refs_2_, ...), custom_call_target="tpu_custom_call", output_to_operand_aliasing={{0}: (11, {})} | custom-call | flops 62914560 | bytes 22020096 | tf_op jit(solution)/shard_map/sweep/pallas_call | solution.py:299
  97.4 2.5 %collective-permute-start.20 = (f32[16,256,128]{2,1,0:T(8,128)S(1)}, f32[16,256,128]{2,1,0:T(8,128)S(1)}, u32[]{:S(2)}, u32[]{:S(2)}) collective-permute-start(f32[16,256,128]{2,1,0:T(8,128)S(1)} %get-tuple-element.52.own), channel_id=1, source_target_pairs={{1,0},{2,1},{3,2},{0,3},{5,4},{6,5},{7,6},{4,7},{9,8},{10,9},{11,1... | collective-permute-start | bytes 6291464 | tf_op jit(solution)/shard_map/ppermute | solution.py:42
  105.2 5.8 %collective-permute-done.11.right = f32[4,256,128]{2,1,0:T(8,128)S(1)} collective-permute-done((f32[4,256,128]{2,1,0:T(8,128)S(1)}, f32[4,256,128]{2,1,0:T(8,128)S(1)}, u32[]{:S(2)}, u32[]{:S(2)}) %collective-permute-start.11) | collective-permute-done | bytes 524320 | tf_op jit(solution)/shard_map/ppermute | solution.py:42
  111.0 2.2 collective-permute-start.17
  113.2 2.9 %collective-permute-done.16.left = f32[4,256,128]{2,1,0:T(8,128)S(1)} collective-permute-done((f32[4,256,128]{2,1,0:T(8,128)S(1)}, f32[4,256,128]{2,1,0:T(8,128)S(1)}, u32[]{:S(2)}, u32[]{:S(2)}) %collective-permute-start.16) | collective-permute-done | bytes 524320 | tf_op jit(solution)/shard_map/ppermute | solution.py:37
  117.7 3.1 %collective-permute-done.17.right = f32[4,256,128]{2,1,0:T(8,128)S(1)} collective-permute-done((f32[4,256,128]{2,1,0:T(8,128)S(1)}, f32[4,256,128]{2,1,0:T(8,128)S(1)}, u32[]{:S(2)}, u32[]{:S(2)}) %collective-permute-start.17) | collective-permute-done | bytes 524320 | tf_op jit(solution)/shard_map/ppermute | solution.py:42
  122.4 3.4 %collective-permute-done.12 = f32[32,32,128]{2,1,0:T(8,128)S(1)} collective-permute-done((f32[32,32,128]{2,1,0:T(8,128)S(1)}, f32[32,32,128]{2,1,0:T(8,128)S(1)}, u32[]{:S(2)}, u32[]{:S(2)}) %collective-permute-start.12) | collective-permute-done | bytes 524320 | tf_op jit(solution)/shard_map/ppermute | solution.py:37
  125.8 5.6 %collective-permute-done.13 = f32[16,32,128]{2,1,0:T(8,128)S(1)} collective-permute-done((f32[16,32,128]{2,1,0:T(8,128)S(1)}, f32[16,32,128]{2,1,0:T(8,128)S(1)}, u32[]{:S(2)}, u32[]{:S(2)}) %collective-permute-start.13) | collective-permute-done | bytes 262176 | tf_op jit(solution)/shard_map/ppermute | solution.py:37
  131.5 10.4 %cone.4.refs_1_.refs_3_ = f32[8,256,128]{2,1,0:T(8,128)S(1)} custom-call(f32[16,256,128]{2,1,0:T(8,128)} %copy-done.4, f32[4,256,128]{2,1,0:T(8,128)S(1)} %collective-permute-done.10.left, f32[4,256,128]{2,1,0:T(8,128)S(1)} %collective-permute-done.11.right, f32[16,32,128]{2,1,0:T(8,128)S(1)} %get-tuple-element.81.above, ...), custom_call_target="tpu_custom_call" | custom-call | flops 9059696640 | bytes 4194304 | tf_op jit(solution)/shard_map/cone/pallas_call | solution.py:413
  142.2 10.3 %cone.5.refs_2_.refs_4_ = f32[8,256,128]{2,1,0:T(8,128)S(1)} custom-call(f32[16,256,128]{2,1,0:T(8,128)} %copy-done.4, f32[4,256,128]{2,1,0:T(8,128)S(1)} %collective-permute-done.10.left, f32[4,256,128]{2,1,0:T(8,128)S(1)} %collective-permute-done.11.right, f32[16,32,128]{2,1,0:T(8,128)S(1)} %get-tuple-element.81.above, ...), custom_call_target="tpu_custom_call" | custom-call | flops 9059696640 | bytes 4194304 | tf_op jit(solution)/shard_map/cone/pallas_call | solution.py:413
  156.8 8.5 %collective-permute-done.21.left = f32[4,256,128]{2,1,0:T(8,128)S(1)} collective-permute-done((f32[4,256,128]{2,1,0:T(8,128)S(1)}, f32[4,256,128]{2,1,0:T(8,128)S(1)}, u32[]{:S(2)}, u32[]{:S(2)}) %collective-permute-start.21) | collective-permute-done | bytes 524320 | tf_op jit(solution)/shard_map/ppermute | solution.py:37
  165.2 2.1 collective-permute-done.22.right
  167.8 20.4 %cone.6.refs_0_.refs_2_ = f32[16,256,128]{2,1,0:T(8,128)} custom-call(f32[16,256,128]{2,1,0:T(8,128)} %copy-done.2, f32[4,256,128]{2,1,0:T(8,128)S(1)} %collective-permute-done.16.left, f32[4,256,128]{2,1,0:T(8,128)S(1)} %copy-done.6, f32[16,32,128]{2,1,0:T(8,128)S(1)} %get-tuple-element.75.above, ...), custom_call_target="tpu_custom_call" | custom-call | flops 18119393280 | bytes 8388608 | tf_op jit(solution)/shard_map/cone/pallas_call | solution.py:413
  188.3 20.5 %cone.7.refs_3_ = f32[16,256,128]{2,1,0:T(8,128)} custom-call(f32[16,256,128]{2,1,0:T(8,128)} %copy-done.3, f32[4,256,128]{2,1,0:T(8,128)S(1)} %collective-permute-done.21.left, f32[4,256,128]{2,1,0:T(8,128)S(1)} %collective-permute-done.22.right, f32[16,32,128]{2,1,0:T(8,128)S(1)} %get-tuple-element.69.above, ...), custom_call_target="tpu_custom_call" | custom-call | flops 18119393280 | bytes 8388608 | tf_op jit(solution)/shard_map/cone/pallas_call | solution.py:413
  208.8 7.0 %step.2.refs_7_ = f32[32,256,128]{2,1,0:T(8,128)} custom-call(f32[16,256,128]{2,1,0:T(8,128)S(1)} %copy-done.1, f32[8,256,128]{2,1,0:T(8,128)S(1)} %cone.4.refs_1_.refs_3_, f32[8,256,128]{2,1,0:T(8,128)S(1)} %cone.5.refs_2_.refs_4_, f32[16,256,128]{2,1,0:T(8,128)} %cone.7.refs_3_, f32[32,256,128]{2,1,0:T(8,128)} %refs_5_.3, s32[32,256,128]{2,1,0:T(8,128)} %refs_6_.1), custom_call_target="tpu_custom_call" | custom-call | flops 6291456 | bytes 12582912 | tf_op jit(solution)/shard_map/step/pallas_call | solution.py:479
  215.8 7.0 %step.3 = f32[32,256,128]{2,1,0:T(8,128)} custom-call(f32[8,256,128]{2,1,0:T(8,128)S(1)} %collective-permute-done.14.refs_0_, f32[8,256,128]{2,1,0:T(8,128)S(1)} %collective-permute-done.15.refs_1_, f32[16,256,128]{2,1,0:T(8,128)} %cone.6.refs_0_.refs_2_, f32[8,256,128]{2,1,0:T(8,128)S(1)} %cone.4.refs_1_.refs_3_, ...), custom_call_target="tpu_custom_call", output_to_operand_aliasing={{}: (7, {})} | custom-call | flops 6291456 | bytes 12582912 | tf_op jit(solution)/shard_map/step/pallas_call | solution.py:479
  (102 shorter events, 26.1 us)
Async XLA Ops:
  1.8 44.2 %collective-permute-start.4 = (f32[3,256,128]{2,1,0:T(8,128)S(1)}, f32[3,256,128]{2,1,0:T(8,128)S(1)}, u32[]{:S(2)}, u32[]{:S(2)}) collective-permute-start(f32[3,256,128]{2,1,0:T(8,128)S(1)} %get-tuple-element.60), channel_id=1, source_target_pairs={{1,0},{2,1},{3,2},{0,3},{5,4},{6,5},{7,6},{4,7},{9,8},{10,9},{11,1... | collective-permute-start | bytes 1179656 | tf_op jit(solution)/shard_map/ppermute | solution.py:42
  6.9 39.1 %collective-permute-start.3 = (f32[3,256,128]{2,1,0:T(8,128)S(1)}, f32[3,256,128]{2,1,0:T(8,128)S(1)}, u32[]{:S(2)}, u32[]{:S(2)}) collective-permute-start(f32[3,256,128]{2,1,0:T(8,128)S(1)} %get-tuple-element.61), channel_id=1, source_target_pairs={{0,1},{1,2},{2,3},{3,0},{4,5},{5,6},{6,7},{7,4},{8,9},{9,10},{10,1... | collective-permute-start | bytes 1179656 | tf_op jit(solution)/shard_map/ppermute | solution.py:37
  17.8 4.7 %collective-permute-start.2 = (f32[192,128]{1,0:T(8,128)S(1)}, f32[192,128]{1,0:T(8,128)S(1)}, u32[]{:S(2)}, u32[]{:S(2)}) collective-permute-start(f32[192,128]{1,0:T(8,128)S(1)} %pad_maximum_fusion.6), channel_id=1, source_target_pairs={{0,4},{4,0},{1,5},{5,1},{2,6},{6,2},{3,7},{7,3},{8,12},{12,8},{9,1... | collective-permute-start | bytes 294920 | tf_op jit(solution)/shard_map/ppermute | solution.py:37
  19.4 4.8 %collective-permute-start.1 = (f32[256,128]{1,0:T(8,128)S(1)}, f32[256,128]{1,0:T(8,128)S(1)}, u32[]{:S(2)}, u32[]{:S(2)}) collective-permute-start(f32[256,128]{1,0:T(8,128)S(1)} %get-tuple-element.31), channel_id=1, source_target_pairs={{8,0},{16,8},{24,16},{0,24},{9,1},{17,9},{25,17},{1,25},{10,2},{18... | collective-permute-start | bytes 393224 | tf_op jit(solution)/shard_map/ppermute | solution.py:42
  56.5 20.1 %collective-permute-start.9 = (f32[3,256,128]{2,1,0:T(8,128)S(1)}, f32[3,256,128]{2,1,0:T(8,128)S(1)}, u32[]{:S(2)}, u32[]{:S(2)}) collective-permute-start(f32[3,256,128]{2,1,0:T(8,128)S(1)} %get-tuple-element.58), channel_id=1, source_target_pairs={{0,1},{1,2},{2,3},{3,0},{4,5},{5,6},{6,7},{7,4},{8,9},{9,10},{10,1... | collective-permute-start | bytes 1179656 | tf_op jit(solution)/shard_map/ppermute | solution.py:37
  56.6 25.6 %collective-permute-start.8 = (f32[3,256,128]{2,1,0:T(8,128)S(1)}, f32[3,256,128]{2,1,0:T(8,128)S(1)}, u32[]{:S(2)}, u32[]{:S(2)}) collective-permute-start(f32[3,256,128]{2,1,0:T(8,128)S(1)} %get-tuple-element.59), channel_id=1, source_target_pairs={{1,0},{2,1},{3,2},{0,3},{5,4},{6,5},{7,6},{4,7},{9,8},{10,9},{11,1... | collective-permute-start | bytes 1179656 | tf_op jit(solution)/shard_map/ppermute | solution.py:42
  60.4 5.6 %collective-permute-start.7 = (f32[192,128]{1,0:T(8,128)S(1)}, f32[192,128]{1,0:T(8,128)S(1)}, u32[]{:S(2)}, u32[]{:S(2)}) collective-permute-start(f32[192,128]{1,0:T(8,128)S(1)} %pad_maximum_fusion.7), channel_id=1, source_target_pairs={{0,4},{4,0},{1,5},{5,1},{2,6},{6,2},{3,7},{7,3},{8,12},{12,8},{9,1... | collective-permute-start | bytes 294920 | tf_op jit(solution)/shard_map/ppermute | solution.py:37
  60.9 5.0 %collective-permute-start.5 = (f32[256,128]{1,0:T(8,128)S(1)}, f32[256,128]{1,0:T(8,128)S(1)}, u32[]{:S(2)}, u32[]{:S(2)}) collective-permute-start(f32[256,128]{1,0:T(8,128)S(1)} %get-tuple-element.40), channel_id=1, source_target_pairs={{0,8},{8,16},{16,24},{24,0},{1,9},{9,17},{17,25},{25,1},{2,10},{10... | collective-permute-start | bytes 393224 | tf_op jit(solution)/shard_map/ppermute | solution.py:37
  61.6 4.4 %collective-permute-start.6 = (f32[256,128]{1,0:T(8,128)S(1)}, f32[256,128]{1,0:T(8,128)S(1)}, u32[]{:S(2)}, u32[]{:S(2)}) collective-permute-start(f32[256,128]{1,0:T(8,128)S(1)} %get-tuple-element.41), channel_id=1, source_target_pairs={{8,0},{16,8},{24,16},{0,24},{9,1},{17,9},{25,17},{1,25},{10,2},{18... | collective-permute-start | bytes 393224 | tf_op jit(solution)/shard_map/ppermute | solution.py:42
  95.9 9.1 %collective-permute-start.10 = (f32[4,256,128]{2,1,0:T(8,128)S(1)}, f32[4,256,128]{2,1,0:T(8,128)S(1)}, u32[]{:S(2)}, u32[]{:S(2)}) collective-permute-start(f32[4,256,128]{2,1,0:T(8,128)S(1)} %get-tuple-element.50), channel_id=1, source_target_pairs={{0,8},{8,16},{16,24},{24,0},{1,9},{9,17},{17,25},{25,1},{2,10},{10... | collective-permute-start | bytes 1572872 | tf_op jit(solution)/shard_map/ppermute | solution.py:37
  97.4 55.2 %collective-permute-start.20 = (f32[16,256,128]{2,1,0:T(8,128)S(1)}, f32[16,256,128]{2,1,0:T(8,128)S(1)}, u32[]{:S(2)}, u32[]{:S(2)}) collective-permute-start(f32[16,256,128]{2,1,0:T(8,128)S(1)} %get-tuple-element.52.own), channel_id=1, source_target_pairs={{1,0},{2,1},{3,2},{0,3},{5,4},{6,5},{7,6},{4,7},{9,8},{10,9},{11,1... | collective-permute-start | bytes 6291464 | tf_op jit(solution)/shard_map/ppermute | solution.py:42
  100.0 22.4 %collective-permute-start.18 = (f32[32,32,128]{2,1,0:T(8,128)S(1)}, f32[32,32,128]{2,1,0:T(8,128)S(1)}, u32[]{:S(2)}, u32[]{:S(2)}) collective-permute-start(f32[32,32,128]{2,1,0:T(8,128)S(1)} %pad_maximum_fusion.1), channel_id=1, source_target_pairs={{0,4},{4,0},{1,5},{5,1},{2,6},{6,2},{3,7},{7,3},{8,12},{12,8},{9,1... | collective-permute-start | bytes 1572872 | tf_op jit(solution)/shard_map/ppermute | solution.py:37
  101.0 10.0 %collective-permute-start.11 = (f32[4,256,128]{2,1,0:T(8,128)S(1)}, f32[4,256,128]{2,1,0:T(8,128)S(1)}, u32[]{:S(2)}, u32[]{:S(2)}) collective-permute-start(f32[4,256,128]{2,1,0:T(8,128)S(1)} %get-tuple-element.51), channel_id=1, source_target_pairs={{8,0},{16,8},{24,16},{0,24},{9,1},{17,9},{25,17},{1,25},{10,2},{18... | collective-permute-start | bytes 1572872 | tf_op jit(solution)/shard_map/ppermute | solution.py:42
  101.7 24.1 %collective-permute-start.12 = (f32[32,32,128]{2,1,0:T(8,128)S(1)}, f32[32,32,128]{2,1,0:T(8,128)S(1)}, u32[]{:S(2)}, u32[]{:S(2)}) collective-permute-start(f32[32,32,128]{2,1,0:T(8,128)S(1)} %pad_maximum_fusion), channel_id=1, source_target_pairs={{0,4},{4,0},{1,5},{5,1},{2,6},{6,2},{3,7},{7,3},{8,12},{12,8},{9,1... | collective-permute-start | bytes 1572872 | tf_op jit(solution)/shard_map/ppermute | solution.py:37
  105.0 11.1 %collective-permute-start.16 = (f32[4,256,128]{2,1,0:T(8,128)S(1)}, f32[4,256,128]{2,1,0:T(8,128)S(1)}, u32[]{:S(2)}, u32[]{:S(2)}) collective-permute-start(f32[4,256,128]{2,1,0:T(8,128)S(1)} %get-tuple-element.53), channel_id=1, source_target_pairs={{0,8},{8,16},{16,24},{24,0},{1,9},{9,17},{17,25},{25,1},{2,10},{10... | collective-permute-start | bytes 1572872 | tf_op jit(solution)/shard_map/ppermute | solution.py:37
  111.0 9.8 %collective-permute-start.17 = (f32[4,256,128]{2,1,0:T(8,128)S(1)}, f32[4,256,128]{2,1,0:T(8,128)S(1)}, u32[]{:S(2)}, u32[]{:S(2)}) collective-permute-start(f32[4,256,128]{2,1,0:T(8,128)S(1)} %get-tuple-element.54), channel_id=1, source_target_pairs={{8,0},{16,8},{24,16},{0,24},{9,1},{17,9},{25,17},{1,25},{10,2},{18... | collective-permute-start | bytes 1572872 | tf_op jit(solution)/shard_map/ppermute | solution.py:42
  116.1 15.3 %collective-permute-start.13 = (f32[16,32,128]{2,1,0:T(8,128)S(1)}, f32[16,32,128]{2,1,0:T(8,128)S(1)}, u32[]{:S(2)}, u32[]{:S(2)}) collective-permute-start(f32[16,32,128]{2,1,0:T(8,128)S(1)} %pad_maximum_fusion.3), channel_id=1, source_target_pairs={{0,4},{4,0},{1,5},{5,1},{2,6},{6,2},{3,7},{7,3},{8,12},{12,8},{9,1... | collective-permute-start | bytes 786440 | tf_op jit(solution)/shard_map/ppermute | solution.py:37
  120.8 33.4 %collective-permute-start.19 = (f32[16,32,128]{2,1,0:T(8,128)S(1)}, f32[16,32,128]{2,1,0:T(8,128)S(1)}, u32[]{:S(2)}, u32[]{:S(2)}) collective-permute-start(f32[16,32,128]{2,1,0:T(8,128)S(1)} %pad_maximum_fusion.4), channel_id=1, source_target_pairs={{0,4},{4,0},{1,5},{5,1},{2,6},{6,2},{3,7},{7,3},{8,12},{12,8},{9,1... | collective-permute-start | bytes 786440 | tf_op jit(solution)/shard_map/ppermute | solution.py:37
  141.9 73.9 %collective-permute-start.14 = (f32[8,256,128]{2,1,0:T(8,128)S(1)}, f32[8,256,128]{2,1,0:T(8,128)S(1)}, u32[]{:S(2)}, u32[]{:S(2)}) collective-permute-start(f32[8,256,128]{2,1,0:T(8,128)S(1)} %cone.4.refs_1_.refs_3_), channel_id=1, source_target_pairs={{0,1},{1,2},{2,3},{3,0},{4,5},{5,6},{6,7},{7,4},{8,9},{9,10},{10,1... | collective-permute-start | bytes 3145736 | tf_op jit(solution)/shard_map/ppermute | solution.py:37
  152.6 63.2 %collective-permute-start.15 = (f32[8,256,128]{2,1,0:T(8,128)S(1)}, f32[8,256,128]{2,1,0:T(8,128)S(1)}, u32[]{:S(2)}, u32[]{:S(2)}) collective-permute-start(f32[8,256,128]{2,1,0:T(8,128)S(1)} %cone.5.refs_2_.refs_4_), channel_id=1, source_target_pairs={{0,1},{1,2},{2,3},{3,0},{4,5},{5,6},{6,7},{7,4},{8,9},{9,10},{10,1... | collective-permute-start | bytes 3145736 | tf_op jit(solution)/shard_map/ppermute | solution.py:37
  153.4 11.8 %collective-permute-start.21 = (f32[4,256,128]{2,1,0:T(8,128)S(1)}, f32[4,256,128]{2,1,0:T(8,128)S(1)}, u32[]{:S(2)}, u32[]{:S(2)}) collective-permute-start(f32[4,256,128]{2,1,0:T(8,128)S(1)} %get-tuple-element.55), channel_id=1, source_target_pairs={{0,8},{8,16},{16,24},{24,0},{1,9},{9,17},{17,25},{25,1},{2,10},{10... | collective-permute-start | bytes 1572872 | tf_op jit(solution)/shard_map/ppermute | solution.py:37
  154.3 13.1 %collective-permute-start.22 = (f32[4,256,128]{2,1,0:T(8,128)S(1)}, f32[4,256,128]{2,1,0:T(8,128)S(1)}, u32[]{:S(2)}, u32[]{:S(2)}) collective-permute-start(f32[4,256,128]{2,1,0:T(8,128)S(1)} %get-tuple-element.56), channel_id=1, source_target_pairs={{8,0},{16,8},{24,16},{0,24},{9,1},{17,9},{25,17},{1,25},{10,2},{18... | collective-permute-start | bytes 1572872 | tf_op jit(solution)/shard_map/ppermute | solution.py:42
  155.4 32.8 %collective-permute-start.23 = (f32[32,32,128]{2,1,0:T(8,128)S(1)}, f32[32,32,128]{2,1,0:T(8,128)S(1)}, u32[]{:S(2)}, u32[]{:S(2)}) collective-permute-start(f32[32,32,128]{2,1,0:T(8,128)S(1)} %pad_maximum_fusion.2), channel_id=1, source_target_pairs={{0,4},{4,0},{1,5},{5,1},{2,6},{6,2},{3,7},{7,3},{8,12},{12,8},{9,1... | collective-permute-start | bytes 1572872 | tf_op jit(solution)/shard_map/ppermute | solution.py:37
  167.4 20.9 %collective-permute-start.24 = (f32[16,32,128]{2,1,0:T(8,128)S(1)}, f32[16,32,128]{2,1,0:T(8,128)S(1)}, u32[]{:S(2)}, u32[]{:S(2)}) collective-permute-start(f32[16,32,128]{2,1,0:T(8,128)S(1)} %pad_maximum_fusion.5), channel_id=1, source_target_pairs={{0,4},{4,0},{1,5},{5,1},{2,6},{6,2},{3,7},{7,3},{8,12},{12,8},{9,1... | collective-permute-start | bytes 786440 | tf_op jit(solution)/shard_map/ppermute | solution.py:37
  (19 other events, 401.6 us)
